TPU v7x, 128 devices: a whole 4x4x4 slice. The times are simulated.
128 devices in a mesh: expert: 32 (over x, y, core), wshard: 4 (over z).
Axes of the slice: x: 4, y: 4, z: 4, core: 2. Of those that a mesh axis runs over, the one named last changes fastest.
Arguments:
- tokens: bfloat16 [24576, 1024], P(('expert', 'wshard')), may hold values from -6 to 6
- w_query: bfloat16 [1024, 1024], P('wshard'), may hold values from -0.75 to 0.75
- w_key: bfloat16 [1024, 512], P('wshard'), may hold values from -0.75 to 0.75
- w_value: bfloat16 [1024, 512], P('wshard'), may hold values from -0.1875 to 0.1875
- w_out: bfloat16 [1024, 1024], P('wshard'), may hold values from -6 to 6
- w_router: bfloat16 [1024, 32], P('wshard'), may hold values from -0.09375 to 0.09375
- gain_attn: bfloat16 [1024], P('wshard'), may hold values from 0.25 to 1.75
- gain_moe: bfloat16 [1024], P('wshard'), may hold values from 0.25 to 1.75
- w_gate: bfloat16 [32, 1024, 512], P('expert'), may hold values from -0.1875 to 0.1875
- w_up: bfloat16 [32, 1024, 512], P('expert'), may hold values from -0.1875 to 0.1875
- w_down: bfloat16 [32, 512, 1024], P('expert'), may hold values from -6 to 6
- routes: int32 [24576, 8], P(('expert', 'wshard')), may hold values from 0 to 31, all different within a row; in each aligned block of 192 rows (0 to 191, 192 to 383, ...) at most 64 rows name the same one
- seq_split: int32 [32], P('expert'), may hold values from 672 to 768, as said below
- cotangent: bfloat16 [24576, 1024], P(('expert', 'wshard')), may hold values from -6 to 6
Outputs:
- output: float32 [24576, 1024], P(('expert', 'wshard'))
- input_grad: float32 [24576, 1024], P(('expert', 'wshard'))
- grad_query: float32 [1024, 1024], P('wshard')
- grad_key: float32 [1024, 512], P('wshard')
- grad_value: float32 [1024, 512], P('wshard')
- grad_out: float32 [1024, 1024], P('wshard')
- grad_router: float32 [1024, 32], P('wshard')
- grad_gain_attn: float32 [1024], P('wshard')
- grad_gain_moe: float32 [1024], P('wshard')
- grad_gate: float32 [32, 1024, 512], P('expert', 'wshard')
- grad_up: float32 [32, 1024, 512], P('expert', 'wshard')
- grad_down: float32 [32, 512, 1024], P('expert', 'wshard')
Inputs may be any that keep to these rules, and one draw needn't show every extreme that they name: `routes`: each row names 8 different experts. Among the 192 rows of one device no expert is named by more than 64 rows, a bound that some block reaches; every expert is named by some row. The first seq_split rows of a group form one sequence and the rest a second one, empty where seq_split is 768; both ends of the range occur in every draw.
All inputs are finite; a program needn't handle non-finite values.
Results may differ from a plain program's by a relative error of at most 0.025.
Values may be sent and summed in bfloat16 or wider, within the bound.
No kernel may reach another device: no remote copies, remote signals or barrier semaphores. Data moves between devices by JAX's collectives and lax.ppermute only.
A program may use at most 192 MiB of HBM per device.

v0:
```python
import jax
import jax.numpy as jnp
from jax import lax
from jax.sharding import PartitionSpec as P

HEADS = 16
KV_HEADS = 8
HEAD_DIM = 64


epsilon = 1e-06
residual_scale = 0.22
score_scale = 0.015625
rope_base = 10000.0
highest = lax.Precision.HIGHEST


def rms_norm(field, gain_value):
    factor = lax.rsqrt(jnp.mean(field * field, axis=-1, keepdims=True) + epsilon)
    return field * factor * gain_value


def rotate(field, position):
    half_dim = field.shape[-1] // 2
    exponent = jnp.arange(half_dim, dtype=jnp.float32) * (2.0 / field.shape[-1])
    frequency = jnp.power(rope_base, -exponent)
    angles = position[:, None] * frequency[None, :]
    cosine = jnp.cos(angles)[:, None, :]
    sine_part = jnp.sin(angles)[:, None, :]
    front_half = field[..., :half_dim]
    back_half = field[..., half_dim:]
    return jnp.concatenate(
        [front_half * cosine - back_half * sine_part, back_half * cosine + front_half * sine_part],
        axis=-1,
    )


def softmax_last(scores):
    return jax.nn.softmax(scores, axis=-1)


def masked_scores(query_b, key_rows, key_mask):
    grouped = query_b.reshape(query_b.shape[0], KV_HEADS, HEADS // KV_HEADS, HEAD_DIM)
    scores = (
        jnp.einsum("qkgd,tkd->kgqt", grouped, key_rows, preferred_element_type=jnp.float32)
        * score_scale
    )
    return jnp.where(key_mask, scores, -1e30)


def local(
    tokens,
    w_query,
    w_key,
    w_value,
    w_out,
    w_router,
    gain_attn,
    gain_moe,
    w_gate,
    w_up,
    w_down,
    routes,
    seq_split,
    cotangent,
):
    row_count = tokens.shape[0]
    model_width = tokens.shape[1]
    lane_count = lax.axis_size("wshard")
    owner_count = lax.axis_size("expert")
    lane_index = lax.axis_index("wshard")
    gathered = (
        lax.all_gather(w_query, "wshard", axis=0, tiled=True),
        lax.all_gather(w_key, "wshard", axis=0, tiled=True),
        lax.all_gather(w_value, "wshard", axis=0, tiled=True),
        lax.all_gather(w_out, "wshard", axis=0, tiled=True),
        lax.all_gather(w_router, "wshard", axis=0, tiled=True),
        lax.all_gather(gain_attn, "wshard", axis=0, tiled=True),
        lax.all_gather(gain_moe, "wshard", axis=0, tiled=True),
    )
    full_query, full_key, full_value, full_out, full_router, full_gain_a, full_gain_m = gathered
    expert_count = full_router.shape[1]
    top_count = routes.shape[1]
    local_experts = w_gate.shape[0]
    capacity = min(row_count, row_count * top_count * 4 // (3 * expert_count))
    group_len = row_count * lane_count
    split_at = seq_split[0]
    places = jnp.arange(group_len, dtype=jnp.int32)
    in_later = places >= split_at
    own_places = lane_index * row_count + jnp.arange(row_count, dtype=jnp.int32)
    own_later = own_places >= split_at
    position = jnp.where(own_later, own_places - split_at, own_places).astype(jnp.float32)
    key_mask = (own_later[:, None] == in_later[None, :]) & (places[None, :] <= own_places[:, None])
    inputs = tokens.astype(jnp.float32)
    normed, first_back = jax.vjp(rms_norm, inputs, full_gain_a.astype(jnp.float32))
    normed_b = normed.astype(jnp.bfloat16)
    query_lin = jnp.dot(normed_b, full_query, preferred_element_type=jnp.float32).reshape(
        row_count, HEADS, HEAD_DIM
    )
    key_lin = jnp.dot(normed_b, full_key, preferred_element_type=jnp.float32).reshape(
        row_count, KV_HEADS, HEAD_DIM
    )
    value_b = (
        jnp.dot(normed_b, full_value, preferred_element_type=jnp.float32)
        .astype(jnp.bfloat16)
        .reshape(row_count, KV_HEADS, HEAD_DIM)
    )

    def turned(piece):
        return rotate(piece, position)

    query_rot, query_back = jax.vjp(turned, query_lin)
    key_rot, key_back = jax.vjp(turned, key_lin)
    query_b = query_rot.astype(jnp.bfloat16)
    key_b = key_rot.astype(jnp.bfloat16)
    key_rows, value_rows = (
        lax.all_gather(key_b, "wshard", axis=0, tiled=True),
        lax.all_gather(value_b, "wshard", axis=0, tiled=True),
    )
    scores = masked_scores(query_b, key_rows, key_mask)
    top_score = jnp.max(scores, axis=-1, keepdims=True)
    expanded = jnp.exp(scores - top_score)
    row_total = jnp.sum(expanded, axis=-1, keepdims=True)
    probs_b = (expanded / row_total).astype(jnp.bfloat16)
    log_total = top_score + jnp.log(row_total)
    mixed = jnp.einsum("kgqt,tkd->qkgd", probs_b, value_rows, preferred_element_type=jnp.float32)
    mixed_b = mixed.reshape(row_count, HEADS * HEAD_DIM).astype(jnp.bfloat16)
    branch = jnp.dot(mixed_b, full_out, preferred_element_type=jnp.float32)
    middle = inputs + residual_scale * branch
    second, second_back = jax.vjp(rms_norm, middle, full_gain_m.astype(jnp.float32))
    second_b = second.astype(jnp.bfloat16)
    logits = jnp.dot(second_b, full_router, preferred_element_type=jnp.float32)
    chosen = jnp.take_along_axis(logits, routes, axis=1)
    gate_probs, gate_back = jax.vjp(softmax_last, chosen)
    expert_ids = jnp.arange(expert_count, dtype=jnp.int32)
    onehot_int = (routes[:, :, None] == expert_ids).astype(jnp.int32)
    per_token = jnp.sum(onehot_int, axis=1)
    before = jnp.cumsum(per_token, axis=0) - per_token
    slot_index = jnp.take_along_axis(before, routes, axis=1)
    dest_slot = (routes * capacity + slot_index).reshape(-1)
    send_shape = (owner_count, local_experts * capacity, model_width)
    buffer_shape = (expert_count * capacity, model_width)
    send_rows = (
        jnp.zeros(buffer_shape, jnp.bfloat16)
        .at[dest_slot]
        .set(jnp.repeat(second_b, top_count, axis=0))
    )
    arrived = lax.all_to_all(
        send_rows.reshape(send_shape), "expert", split_axis=0, concat_axis=0, tiled=True
    )
    rows_in = arrived.reshape(owner_count, local_experts, capacity, model_width)
    gate_lin = jnp.einsum("sxcd,xdf->sxcf", rows_in, w_gate, preferred_element_type=jnp.float32)
    up_lin = jnp.einsum("sxcd,xdf->sxcf", rows_in, w_up, preferred_element_type=jnp.float32)
    activated, silu_back = jax.vjp(jax.nn.silu, gate_lin)
    hidden_b = (activated * up_lin).astype(jnp.bfloat16)
    expert_out = jnp.einsum(
        "sxcf,xfd->sxcd", hidden_b, w_down, preferred_element_type=jnp.float32
    ).astype(jnp.bfloat16)
    returned = lax.all_to_all(
        expert_out.reshape(send_shape), "expert", split_axis=0, concat_axis=0, tiled=True
    )
    picked = (
        jnp.take(returned.reshape(buffer_shape), dest_slot, axis=0)
        .reshape(row_count, top_count, model_width)
        .astype(jnp.float32)
    )
    expert_sum = jnp.einsum("tk,tkd->td", gate_probs, picked, precision=highest)
    output = middle + residual_scale * expert_sum
    upstream = cotangent.astype(jnp.float32)
    scaled = residual_scale * upstream
    picked_grad = (gate_probs[:, :, None] * scaled[:, None, :]).astype(jnp.bfloat16)
    gate_grad = jnp.einsum("td,tkd->tk", scaled, picked, precision=highest)
    chosen_grad = gate_back(gate_grad)[0]
    logit_grad = jnp.einsum(
        "tk,tke->te", chosen_grad, onehot_int.astype(jnp.float32), precision=highest
    )
    send_grad = (
        jnp.zeros(buffer_shape, jnp.bfloat16)
        .at[dest_slot]
        .set(picked_grad.reshape(-1, model_width))
    )
    grad_in = lax.all_to_all(
        send_grad.reshape(send_shape), "expert", split_axis=0, concat_axis=0, tiled=True
    )
    grad_in = grad_in.reshape(owner_count, local_experts, capacity, model_width)
    hidden_grad = jnp.einsum(
        "sxcd,xfd->sxcf", grad_in, w_down, preferred_element_type=jnp.float32
    ).astype(jnp.bfloat16)
    down_grad = jnp.einsum("sxcf,sxcd->xfd", hidden_b, grad_in, preferred_element_type=jnp.float32)
    hidden_float = hidden_grad.astype(jnp.float32)
    gate_lin_grad = silu_back(hidden_float * up_lin)[0].astype(jnp.bfloat16)
    up_lin_grad = (hidden_float * activated).astype(jnp.bfloat16)
    gate_weight_grad = jnp.einsum(
        "sxcd,sxcf->xdf", rows_in, gate_lin_grad, preferred_element_type=jnp.float32
    )
    up_weight_grad = jnp.einsum(
        "sxcd,sxcf->xdf", rows_in, up_lin_grad, preferred_element_type=jnp.float32
    )
    row_grad = jnp.einsum(
        "sxcf,xdf->sxcd", gate_lin_grad, w_gate, preferred_element_type=jnp.float32
    )
    row_grad = (
        row_grad
        + jnp.einsum("sxcf,xdf->sxcd", up_lin_grad, w_up, preferred_element_type=jnp.float32)
    ).astype(jnp.bfloat16)
    row_back = lax.all_to_all(
        row_grad.reshape(send_shape), "expert", split_axis=0, concat_axis=0, tiled=True
    )
    gathered_grad = jnp.take(row_back.reshape(buffer_shape), dest_slot, axis=0).reshape(
        row_count, top_count, model_width
    )
    second_grad = jnp.sum(gathered_grad.astype(jnp.float32), axis=1)
    router_float = full_router.astype(jnp.float32)
    second_grad = second_grad + jnp.dot(logit_grad, router_float.T, precision=highest)
    router_grad = jnp.dot(second_b.astype(jnp.float32).T, logit_grad, precision=highest)
    middle_norm_grad, gain_m_grad = second_back(second_grad)
    middle_grad = upstream + middle_norm_grad
    branch_grad = (residual_scale * middle_grad).astype(jnp.bfloat16)
    out_grad = jnp.dot(mixed_b.T, branch_grad, preferred_element_type=jnp.float32)
    mixed_grad = jnp.dot(branch_grad, full_out.T, preferred_element_type=jnp.float32).astype(
        jnp.bfloat16
    )
    mixed_grad = mixed_grad.reshape(row_count, KV_HEADS, HEADS // KV_HEADS, HEAD_DIM)
    back_keys, back_values = (key_rows, value_rows)
    scores_again = masked_scores(query_b, back_keys, key_mask)
    probs = jnp.exp(scores_again - log_total)
    probs_again = probs.astype(jnp.bfloat16)
    prob_grad = jnp.einsum(
        "qkgd,tkd->kgqt", mixed_grad, back_values, preferred_element_type=jnp.float32
    )
    value_grad = jnp.einsum(
        "kgqt,qkgd->tkd", probs_again, mixed_grad, preferred_element_type=jnp.float32
    )
    score_grad = (probs * (prob_grad - jnp.sum(probs * prob_grad, axis=-1, keepdims=True))).astype(
        jnp.bfloat16
    )
    grouped = query_b.reshape(row_count, KV_HEADS, HEADS // KV_HEADS, HEAD_DIM)
    query_grad = (
        jnp.einsum("kgqt,tkd->qkgd", score_grad, back_keys, preferred_element_type=jnp.float32)
        * score_scale
    )
    query_grad = query_grad.reshape(row_count, HEADS, HEAD_DIM)
    key_grad = (
        jnp.einsum("kgqt,qkgd->tkd", score_grad, grouped, preferred_element_type=jnp.float32)
        * score_scale
    )
    key_own, value_own = (
        lax.psum_scatter(
            key_grad.astype(jnp.bfloat16), "wshard", scatter_dimension=0, tiled=True
        ).astype(jnp.float32),
        lax.psum_scatter(
            value_grad.astype(jnp.bfloat16), "wshard", scatter_dimension=0, tiled=True
        ).astype(jnp.float32),
    )
    query_lin_grad = (
        query_back(query_grad)[0].astype(jnp.bfloat16).reshape(row_count, HEADS * HEAD_DIM)
    )
    key_lin_grad = key_back(key_own)[0].astype(jnp.bfloat16).reshape(row_count, KV_HEADS * HEAD_DIM)
    value_lin_grad = value_own.astype(jnp.bfloat16).reshape(row_count, KV_HEADS * HEAD_DIM)
    query_weight_grad = jnp.dot(normed_b.T, query_lin_grad, preferred_element_type=jnp.float32)
    key_weight_grad = jnp.dot(normed_b.T, key_lin_grad, preferred_element_type=jnp.float32)
    value_weight_grad = jnp.dot(normed_b.T, value_lin_grad, preferred_element_type=jnp.float32)
    normed_grad = jnp.dot(query_lin_grad, full_query.T, preferred_element_type=jnp.float32)
    normed_grad = normed_grad + jnp.dot(
        key_lin_grad, full_key.T, preferred_element_type=jnp.float32
    )
    normed_grad = normed_grad + jnp.dot(
        value_lin_grad, full_value.T, preferred_element_type=jnp.float32
    )
    input_norm_grad, gain_a_grad = first_back(normed_grad)
    input_grad = middle_grad + input_norm_grad
    summed = (
        lax.psum(query_weight_grad.astype(jnp.bfloat16), "expert").astype(jnp.float32),
        lax.psum(key_weight_grad.astype(jnp.bfloat16), "expert").astype(jnp.float32),
        lax.psum(value_weight_grad.astype(jnp.bfloat16), "expert").astype(jnp.float32),
        lax.psum(out_grad.astype(jnp.bfloat16), "expert").astype(jnp.float32),
        lax.psum(router_grad.astype(jnp.bfloat16), "expert").astype(jnp.float32),
        lax.psum(gain_a_grad.astype(jnp.bfloat16), "expert").astype(jnp.float32),
        lax.psum(gain_m_grad.astype(jnp.bfloat16), "expert").astype(jnp.float32),
    )
    shares = (
        lax.psum_scatter(
            summed[0].astype(jnp.bfloat16), "wshard", scatter_dimension=0, tiled=True
        ).astype(jnp.float32),
        lax.psum_scatter(
            summed[1].astype(jnp.bfloat16), "wshard", scatter_dimension=0, tiled=True
        ).astype(jnp.float32),
        lax.psum_scatter(
            summed[2].astype(jnp.bfloat16), "wshard", scatter_dimension=0, tiled=True
        ).astype(jnp.float32),
        lax.psum_scatter(
            summed[3].astype(jnp.bfloat16), "wshard", scatter_dimension=0, tiled=True
        ).astype(jnp.float32),
        lax.psum_scatter(
            summed[4].astype(jnp.bfloat16), "wshard", scatter_dimension=0, tiled=True
        ).astype(jnp.float32),
        lax.psum_scatter(
            summed[5].astype(jnp.bfloat16), "wshard", scatter_dimension=0, tiled=True
        ).astype(jnp.float32),
        lax.psum_scatter(
            summed[6].astype(jnp.bfloat16), "wshard", scatter_dimension=0, tiled=True
        ).astype(jnp.float32),
    )
    gate_share, up_share, down_share = (
        lax.psum_scatter(
            gate_weight_grad.astype(jnp.bfloat16), "wshard", scatter_dimension=1, tiled=True
        ).astype(jnp.float32),
        lax.psum_scatter(
            up_weight_grad.astype(jnp.bfloat16), "wshard", scatter_dimension=1, tiled=True
        ).astype(jnp.float32),
        lax.psum_scatter(
            down_grad.astype(jnp.bfloat16), "wshard", scatter_dimension=1, tiled=True
        ).astype(jnp.float32),
    )
    return (
        output,
        input_grad,
        shares[0],
        shares[1],
        shares[2],
        shares[3],
        shares[4],
        shares[5],
        shares[6],
        gate_share,
        up_share,
        down_share,
    )


def solution(mesh):
    in_specs = (
        P(("expert", "wshard"), None),
        P("wshard", None),
        P("wshard", None),
        P("wshard", None),
        P("wshard", None),
        P("wshard", None),
        P("wshard"),
        P("wshard"),
        P("expert", None, None),
        P("expert", None, None),
        P("expert", None, None),
        P(("expert", "wshard"), None),
        P("expert"),
        P(("expert", "wshard"), None),
    )
    out_specs = (
        P(("expert", "wshard"), None),
        P(("expert", "wshard"), None),
        P("wshard", None),
        P("wshard", None),
        P("wshard", None),
        P("wshard", None),
        P("wshard", None),
        P("wshard"),
        P("wshard"),
        P("expert", "wshard", None),
        P("expert", "wshard", None),
        P("expert", "wshard", None),
    )
    return jax.shard_map(local, mesh=mesh, in_specs=in_specs, out_specs=out_specs, check_vma=False)
```

profile of v0, /device:TPU:0, one launch (start us, length us, event | category | flops | bytes accessed | tf_op | source)
XLA Modules:
  0.0 864.9 jit_solution(2239475592274012035)
XLA Ops:
  14.7 11.1 %all-gather.1 = bf16[4,1,256]{2,1,0:T(2,128)(2,1)S(1)} all-gather(bf16[1,1,256]{2,1,0:T(2,128)(2,1)S(1)} %reshape.429), channel_id=1, replica_groups=mesh['expert'=32,'wshard'=4] {'wshard'}, dimensions={0}, use_global_device_ids=true | all-gather | bytes 2560 | tf_op jit(solution)/shard_map/all_gather | solution.py:79
  25.7 7.0 all-gather
  33.7 12.9 %all_gather.35 = bf16[1024,32]{0,1:T(8,128)(2,1)} all-gather(bf16[256,32]{0,1:T(8,128)(2,1)} %param.21), channel_id=1, replica_groups=mesh['expert'=32,'wshard'=4] {'wshard'}, dimensions={0}, use_global_device_ids=true | all-gather | bytes 81920 | tf_op jit(solution)/shard_map/all_gather | solution.py:77
  47.0 10.3 %gather_fusion.1 = s32[1536]{0:T(1024)S(1)} fusion(s32[192,32]{1,0:T(8,128)S(1)} %slice_subtract_fusion, s32[1536]{0:T(1024)S(1)} %reshape.392), kind=kCustom, calls=%fused_computation.3 | custom fusion | bytes 24576 | tf_op jit(solution)/shard_map/jit(take_along_axis)/gather | solution.py:139
  65.1 20.4 %all_gather.31 = bf16[768,8,64]{2,1,0:T(8,128)(2,1)} all-gather(bf16[192,8,64]{2,1,0:T(8,128)(2,1)S(1)} %copy.100), channel_id=1, replica_groups=mesh['expert'=32,'wshard'=4] {'wshard'}, dimensions={0}, use_global_device_ids=true | all-gather | bytes 983040 | tf_op jit(solution)/shard_map/all_gather | solution.py:117
  87.5 25.2 %all_gather.29 = bf16[768,8,64]{2,1,0:T(8,128)(2,1)} all-gather(bf16[192,8,64]{2,1,0:T(8,128)(2,1)S(1)} %copy.98), channel_id=1, replica_groups=mesh['expert'=32,'wshard'=4] {'wshard'}, dimensions={0}, use_global_device_ids=true | all-gather | bytes 983040 | tf_op jit(solution)/shard_map/all_gather | solution.py:118
  123.6 3.8 fusion.48
  127.4 12.4 %all-gather.13.cloned.1.call-done = bf16[1024,1024]{1,0:T(8,128)(2,1)} async-done(((bf16[256,1024]{1,0:T(8,128)(2,1)}), bf16[1024,1024]{1,0:T(8,128)(2,1)}) %all-gather.13.cloned.1.call-update) | async-done | bytes 2097168 | tf_op jit(solution)/shard_map/all_gather | solution.py:76
  143.3 12.7 %gather_fusion = f32[1536]{0:T(1024)S(1)} fusion(f32[192,32]{0,1:T(8,128)S(1)} %fusion.105, s32[1536]{0:T(1024)S(1)} %reshape.392), kind=kCustom, calls=%fused_computation.2 | custom fusion | bytes 24576 | tf_op jit(solution)/shard_map/jit(take_along_axis)/gather | solution.py:133
  161.4 11.2 %scatter_custom_fusion.1 = bf16[2048,1024]{1,0:T(8,128)(2,1)} fusion(s32[1536]{0:T(1024)} %fusion.75, f32[192,1024]{1,0:T(8,128)S(1)} %copy-done.13, f32[1536]{0:T(1024)S(1)} %mul.399, bf16[]{:T(256)} %constant.53.clone.1), kind=kCustom, calls=%fused_computation.40 | custom fusion | flops 3145728 | bytes 4987392 | tf_op jit(solution)/shard_map/scatter | solution.py:180
  172.6 7.2 all-to-all-start.2
  179.9 10.3 %scatter_custom_fusion = bf16[2048,1024]{1,0:T(8,128)(2,1)} fusion(s32[1536]{0:T(1024)} %fusion.75, bf16[]{:T(256)} %constant.53.clone.1, bf16[192,1024]{1,0:T(8,128)(2,1)S(1)} %multiply_convert_fusion.1), kind=kCustom, calls=%fused_computation.45 | custom fusion | bytes 4588032 | tf_op jit(solution)/shard_map/scatter | solution.py:146
  190.2 42.5 %all-to-all-done.2 = bf16[32,64,1024]{2,1,0:T(8,128)(2,1)} async-done(((bf16[32,64,1024]{2,1,0:T(8,128)(2,1)}), bf16[32,64,1024]{2,1,0:T(8,128)(2,1)}, u32[]{:S(2)}, u32[]{:S(2)}) %all-to-all-start.2) | async-done | bytes 4194336 | tf_op jit(solution)/shard_map/all_to_all | solution.py:182
  232.7 6.9 all-to-all-start
  239.5 6.2 convolution_convert_fusion.1
  245.7 46.5 %all-to-all-done = bf16[32,64,1024]{2,1,0:T(8,128)(2,1)} async-done(((bf16[32,64,1024]{2,1,0:T(8,128)(2,1)}), bf16[32,64,1024]{2,1,0:T(8,128)(2,1)}, u32[]{:S(2)}, u32[]{:S(2)}) %all-to-all-start) | async-done | bytes 4194336 | tf_op jit(solution)/shard_map/all_to_all | solution.py:148
  292.3 5.0 fusion.55
  297.3 8.8 %fusion.13 = (bf16[32,1,64,512]{3,2,0,1:T(8,128)(2,1)}, bf16[32,64,512]{2,1,0:T(8,128)(2,1)S(1)}) fusion(f32[32,64,512]{2,1,0:T(8,128)S(1)} %fusion.55, bf16[32,64,512]{2,1,0:T(8,128)(2,1)S(1)} %copy-done.60, bf16[32,64,1024]{2,1,0:T(8,128)(2,1)} %all-to-all-done, bf16[1,1024,512]{2,1,0:T(8,128)(2,1)S(1)} %copy-done), kind=kOutput, calls=%fused_computation.30 | convolution fusion | flops 2163212288 | bytes 15728640 | tf_op jit(solution)/shard_map/sxcd,xdf->sxcf/dot_general | solution.py:153
  307.4 4.4 convolution_convert_fusion
  311.9 7.1 all-to-all-start.1
  319.0 4.5 fusion.33
  323.5 5.0 add_convert_fusion
  328.5 43.2 %all-to-all-done.1 = bf16[32,64,1024]{2,1,0:T(8,128)(2,1)} async-done(((bf16[32,64,1024]{2,1,0:T(8,128)(2,1)}), bf16[32,64,1024]{2,1,0:T(8,128)(2,1)}, u32[]{:S(2)}, u32[]{:S(2)}) %all-to-all-start.1) | async-done | bytes 4194336 | tf_op jit(solution)/shard_map/all_to_all | solution.py:159
  371.7 6.6 all-to-all-start.3
  378.7 10.8 %gather_fusion.2 = bf16[1536,1024]{1,0:T(8,128)(2,1)} fusion(bf16[2048,1024]{1,0:T(8,128)(2,1)} %bitcast.35, s32[2048]{0:T(1024)S(1)} %pad_clamp_fusion), kind=kCustom, calls=%fused_computation.clone | custom fusion | bytes 6297600 | tf_op jit(solution)/shard_map/jit(_take)/gather | solution.py:163
  389.5 8.6 fusion.21
  398.4 5.5 fusion.23
  403.9 27.3 %all-to-all-done.3 = bf16[32,64,1024]{2,1,0:T(8,128)(2,1)} async-done(((bf16[32,64,1024]{2,1,0:T(8,128)(2,1)}), bf16[32,64,1024]{2,1,0:T(8,128)(2,1)}, u32[]{:S(2)}, u32[]{:S(2)}) %all-to-all-start.3) | async-done | bytes 4194336 | tf_op jit(solution)/shard_map/all_to_all | solution.py:206
  431.1 10.6 %gather_fusion.3 = bf16[1536,1024]{1,0:T(8,128)(2,1)} fusion(bf16[2048,1024]{1,0:T(8,128)(2,1)} %bitcast.49, s32[2048]{0:T(1024)S(1)} %pad_clamp_fusion), kind=kCustom, calls=%fused_computation.1.clone | custom fusion | bytes 6297600 | tf_op jit(solution)/shard_map/jit(_take)/gather | solution.py:209
  441.7 3.9 convert_reduce_fusion
  448.8 6.2 bitcast_convert_fusion.3
  457.4 6.2 fusion
  463.6 5.7 fusion.2
  473.8 7.5 fusion.46
  481.3 6.2 fusion.47
  487.9 6.2 fusion.43
  496.9 7.7 reduce-scatter.31.cloned.1.call-done
  509.6 3.9 convolution_multiply_fusion
  517.3 12.9 %reduce-scatter.17.cloned.1.call-done = bf16[1,256,512]{2,1,0:T(8,128)(2,1)} async-done(((bf16[1,1024,512]{2,1,0:T(8,128)(2,1)}), bf16[1,256,512]{2,1,0:T(8,128)(2,1)}) %reduce-scatter.17.cloned.1.call-update) | async-done | bytes 262160 | tf_op jit(solution)/shard_map/reduce_scatter | solution.py:308
  532.1 24.0 %reduce-scatter.19.cloned.1.call-done = bf16[1,128,1024]{2,1,0:T(8,128)(2,1)} async-done(((bf16[1,512,1024]{2,1,0:T(8,128)(2,1)}), bf16[1,128,1024]{2,1,0:T(8,128)(2,1)}) %reduce-scatter.19.cloned.1.call-update) | async-done | bytes 262160 | tf_op jit(solution)/shard_map/reduce_scatter | solution.py:311
  557.9 24.0 %reduce-scatter.15.cloned.1.call-done = bf16[1,256,512]{2,1,0:T(8,128)(2,1)} async-done(((bf16[1,1024,512]{2,1,0:T(8,128)(2,1)}), bf16[1,256,512]{2,1,0:T(8,128)(2,1)}) %reduce-scatter.15.cloned.1.call-update) | async-done | bytes 262160 | tf_op jit(solution)/shard_map/reduce_scatter | solution.py:305
  588.6 19.6 %reduce-scatter.25.cloned.1.call-done = bf16[256,512]{1,0:T(8,128)(2,1)} async-done(((bf16[1024,512]{1,0:T(8,128)(2,1)}), bf16[256,512]{1,0:T(8,128)(2,1)}) %reduce-scatter.25.cloned.1.call-update) | async-done | bytes 262160 | tf_op jit(solution)/shard_map/reduce_scatter | solution.py:288
  608.1 26.3 %reduce-scatter.23.cloned.1.call-done = bf16[256,512]{1,0:T(8,128)(2,1)} async-done(((bf16[1024,512]{1,0:T(8,128)(2,1)}), bf16[256,512]{1,0:T(8,128)(2,1)}) %reduce-scatter.23.cloned.1.call-update) | async-done | bytes 262160 | tf_op jit(solution)/shard_map/reduce_scatter | solution.py:285
  634.4 31.9 %reduce-scatter.27.cloned.1.call-done = bf16[256,1024]{1,0:T(8,128)(2,1)} async-done(((bf16[1024,1024]{1,0:T(8,128)(2,1)}), bf16[256,1024]{1,0:T(8,128)(2,1)}) %reduce-scatter.27.cloned.1.call-update) | async-done | bytes 524304 | tf_op jit(solution)/shard_map/reduce_scatter | solution.py:291
  666.3 31.9 %reduce-scatter.21.cloned.1.call-done = bf16[256,1024]{1,0:T(8,128)(2,1)} async-done(((bf16[1024,1024]{1,0:T(8,128)(2,1)}), bf16[256,1024]{1,0:T(8,128)(2,1)}) %reduce-scatter.21.cloned.1.call-update) | async-done | bytes 524304 | tf_op jit(solution)/shard_map/reduce_scatter | solution.py:282
  700.5 8.5 all-reduce.9
  709.2 12.1 %reduce-scatter.29.cloned.1.call-done = bf16[256,32]{0,1:T(8,128)(2,1)} async-done(((bf16[1024,32]{0,1:T(8,128)(2,1)}), bf16[256,32]{0,1:T(8,128)(2,1)}) %reduce-scatter.29.cloned.1.call-update) | async-done | bytes 16400 | tf_op jit(solution)/shard_map/reduce_scatter | solution.py:294
  721.3 125.9 %all-reduce.7 = (bf16[256,32]{0,1:T(8,128)(2,1)S(1)}, bf16[256]{0:T(256)(128)(2,1)S(1)}, bf16[256]{0:T(256)(128)(2,1)S(1)}) all-reduce(bf16[256,32]{0,1:T(8,128)(2,1)} %reduce-scatter.29.cloned.1.call-done, bf16[256]{0:T(256)(128)(2,1)S(1)} %dynamic-slice.1, ...), channel_id=1, replica_groups=mesh['expert'=32,'wshard'=4] {'expert'}, use_global_device_ids=true, to_apply=%region_26.28 | all-reduce | flops 8704 | bytes 34816 | tf_op jit(solution)/shard_map/psum | solution.py:277
  (265 shorter events, 83.3 us)
Async XLA Ops:
  7.2 290.1 %copy-start = (bf16[1,1024,512]{2,1,0:T(8,128)(2,1)S(1)}, bf16[1,1024,512]{2,1,0:T(8,128)(2,1)}, u32[]{:S(2)}) copy-start(bf16[1,1024,512]{2,1,0:T(8,128)(2,1)} %param.25) | copy-start | bytes 3145732
  7.2 53.6 %all-gather.7.cloned.1.call-start = ((), (), s32[]{:S(2)}) async-start(), calls=%async_computation.14 | async-start | bytes 1310720 | tf_op jit(solution)/shard_map/all_gather | solution.py:75
  7.9 55.0 %all-gather.9.cloned.1.call-start = ((), (), s32[]{:S(2)}) async-start(), calls=%async_computation.15 | async-start | bytes 1310720 | tf_op jit(solution)/shard_map/all_gather | solution.py:74
  8.7 106.1 %all-gather.11.cloned.1.call-start = ((), (), s32[]{:S(2)}) async-start(), calls=%async_computation.16 | async-start | bytes 2621440 | tf_op jit(solution)/shard_map/all_gather | solution.py:73
  9.4 130.4 %all-gather.13.cloned.1.call-start = ((), (), s32[]{:S(2)}) async-start(), calls=%async_computation.17 | async-start | bytes 2621440 | tf_op jit(solution)/shard_map/all_gather | solution.py:76
  13.3 101.5 %copy-start.43 = (f32[192]{0:T(256)}, f32[192]{0:T(256)S(1)}, u32[]{:S(2)}) copy-start(f32[192]{0:T(256)S(1)} %fusion.80) | copy-start | bytes 2308
  25.7 116.6 %copy-start.39 = (f32[4,1,256]{2,1,0:T(1,128)}, f32[4,1,256]{2,1,0:T(1,128)S(1)}, u32[]{:S(2)}) copy-start(f32[4,1,256]{2,1,0:T(1,128)S(1)} %convert_element_type.285) | copy-start | bytes 12292
  32.7 82.1 %copy-start.31 = (f32[4,1,256]{2,1,0:T(1,128)}, f32[4,1,256]{2,1,0:T(1,128)S(1)}, u32[]{:S(2)}) copy-start(f32[4,1,256]{2,1,0:T(1,128)S(1)} %convert_element_type.284) | copy-start | bytes 12292
  47.0 10.6 %copy-start.36 = (s32[192,8]{0,1:T(8,128)S(1)}, s32[192,8]{0,1:T(8,128)}, u32[]{:S(2)}) copy-start(s32[192,8]{0,1:T(8,128)} %param.27) | copy-start | bytes 18436
  47.0 12.0 %copy-start.21 = (bf16[192,1024]{1,0:T(8,128)(2,1)S(1)}, bf16[192,1024]{1,0:T(8,128)(2,1)}, u32[]{:S(2)}) copy-start(bf16[192,1024]{1,0:T(8,128)(2,1)} %param.29) | copy-start | bytes 1179652
  47.0 13.8 %copy-start.4 = (bf16[192,1024]{1,0:T(8,128)(2,1)S(1)}, bf16[192,1024]{1,0:T(8,128)(2,1)}, u32[]{:S(2)}) copy-start(bf16[192,1024]{1,0:T(8,128)(2,1)} %param.16) | copy-start | bytes 1179652
  60.5 57.1 %copy-start.23 = (f32[192,32]{0,1:T(8,128)}, f32[192,32]{0,1:T(8,128)S(1)}, u32[]{:S(2)}) copy-start(f32[192,32]{0,1:T(8,128)S(1)} %get-tuple-element.42) | copy-start | bytes 73732
  60.5 57.1 %copy-start.25 = (f32[192,32]{0,1:T(8,128)}, f32[192,32]{0,1:T(8,128)S(1)}, u32[]{:S(2)}) copy-start(f32[192,32]{0,1:T(8,128)S(1)} %get-tuple-element.43) | copy-start | bytes 73732
  60.8 61.7 %copy-start.9 = (pred[192,768]{1,0:T(8,128)(4,1)}, pred[192,768]{1,0:T(8,128)(4,1)S(1)}, u32[]{:S(2)}) copy-start(pred[192,768]{1,0:T(8,128)(4,1)S(1)} %fusion.66) | copy-start | bytes 442372
  87.5 30.3 %copy-start.6 = (bf16[768,8,64,1]{0,2,3,1:T(8,128)(2,1)}, bf16[768,8,64,1]{0,2,3,1:T(8,128)(2,1)S(1)}, u32[]{:S(2)}) copy-start(bf16[768,8,64,1]{0,2,3,1:T(8,128)(2,1)S(1)} %copy.119) | copy-start | bytes 2359300
  127.4 15.6 %copy-start.29 = (bf16[1024,32]{0,1:T(8,128)(2,1)S(1)}, bf16[1024,32]{0,1:T(8,128)(2,1)}, u32[]{:S(2)}) copy-start(bf16[1024,32]{0,1:T(8,128)(2,1)} %all_gather.35) | copy-start | bytes 196612
  143.3 18.2 %copy-start.13 = (f32[192,1024]{1,0:T(8,128)S(1)}, f32[192,1024]{1,0:T(8,128)}, u32[]{:S(2)}) copy-start(f32[192,1024]{1,0:T(8,128)} %get-tuple-element.41) | copy-start | bytes 2359300
  172.6 60.0 %all-to-all-start.2 = ((bf16[32,64,1024]{2,1,0:T(8,128)(2,1)}), bf16[32,64,1024]{2,1,0:T(8,128)(2,1)}, u32[]{:S(2)}, u32[]{:S(2)}) async-start(bf16[32,64,1024]{2,1,0:T(8,128)(2,1)} %bitcast.271), calls=%async_computation.2 | async-start | bytes 8388608 | tf_op jit(solution)/shard_map/all_to_all | solution.py:182
  232.7 59.6 %all-to-all-start = ((bf16[32,64,1024]{2,1,0:T(8,128)(2,1)}), bf16[32,64,1024]{2,1,0:T(8,128)(2,1)}, u32[]{:S(2)}, u32[]{:S(2)}) async-start(bf16[32,64,1024]{2,1,0:T(8,128)(2,1)} %bitcast.272), calls=%async_computation | async-start | bytes 8388608 | tf_op jit(solution)/shard_map/all_to_all | solution.py:148
  297.3 10.1 %copy-start.55 = (bf16[1,512,1024]{2,1,0:T(8,128)(2,1)S(1)}, bf16[1,512,1024]{2,1,0:T(8,128)(2,1)}, u32[]{:S(2)}) copy-start(bf16[1,512,1024]{2,1,0:T(8,128)(2,1)} %param.26) | copy-start | bytes 3145732
  311.9 59.8 %all-to-all-start.1 = ((bf16[32,64,1024]{2,1,0:T(8,128)(2,1)}), bf16[32,64,1024]{2,1,0:T(8,128)(2,1)}, u32[]{:S(2)}, u32[]{:S(2)}) async-start(bf16[32,64,1024]{2,1,0:T(8,128)(2,1)} %convolution_convert_fusion), calls=%async_computation.1 | async-start | bytes 8388608 | tf_op jit(solution)/shard_map/all_to_all | solution.py:159
  328.5 50.1 %copy-start.50 = (f32[192]{0:T(256)S(1)}, f32[192]{0:T(256)}, u32[]{:S(2)}) copy-start(f32[192]{0:T(256)} %copy-done.49) | copy-start | bytes 2308
  328.5 50.2 %copy-start.35 = (f32[8,2,192]{2,1,0:T(2,128)S(1)}, f32[8,2,192]{2,1,0:T(2,128)}, u32[]{:S(2)}) copy-start(f32[8,2,192]{2,1,0:T(2,128)} %copy-done.34) | copy-start | bytes 36868
  328.5 50.2 %copy-start.42 = (f32[8,2,192]{2,1,0:T(2,128)S(1)}, f32[8,2,192]{2,1,0:T(2,128)}, u32[]{:S(2)}) copy-start(f32[8,2,192]{2,1,0:T(2,128)} %copy-done.41) | copy-start | bytes 36868
  371.7 59.4 %all-to-all-start.3 = ((bf16[32,64,1024]{2,1,0:T(8,128)(2,1)}), bf16[32,64,1024]{2,1,0:T(8,128)(2,1)}, u32[]{:S(2)}, u32[]{:S(2)}) async-start(bf16[32,64,1024]{2,1,0:T(8,128)(2,1)} %add_convert_fusion), calls=%async_computation.3 | async-start | bytes 8388608 | tf_op jit(solution)/shard_map/all_to_all | solution.py:206
  378.3 115.9 %reduce-scatter.33.cloned.1.call-start = ((), (), s32[]{:S(2)}) async-start(), calls=%async_computation.27 | async-start | bytes 983040 | tf_op jit(solution)/shard_map/reshape | solution.py:259
  378.7 10.8 %copy-start.28 = (f32[192,1024,1]{1,0,2:T(8,128)S(1)}, f32[192,1024,1]{1,0,2:T(8,128)}, u32[]{:S(2)}) copy-start(f32[192,1024,1]{1,0,2:T(8,128)} %get-tuple-element.40) | copy-start | bytes 2359300
  431.1 14.5 %copy-start.30 = (bf16[1024,32]{0,1:T(8,128)(2,1)S(1)}, bf16[1024,32]{0,1:T(8,128)(2,1)}, u32[]{:S(2)}) copy-start(bf16[1024,32]{0,1:T(8,128)(2,1)} %all_gather.35) | copy-start | bytes 196612
  431.1 14.5 %copy-start.40 = (f32[4,1,256]{2,1,0:T(1,128)S(1)}, f32[4,1,256]{2,1,0:T(1,128)}, u32[]{:S(2)}) copy-start(f32[4,1,256]{2,1,0:T(1,128)} %copy-done.39) | copy-start | bytes 12292
  431.1 14.5 %copy-start.48 = (f32[192]{0:T(256)S(1)}, f32[192]{0:T(256)}, u32[]{:S(2)}) copy-start(f32[192]{0:T(256)} %copy-done.47) | copy-start | bytes 2308
  457.3 47.2 %reduce-scatter.31.cloned.1.call-start = ((), (), s32[]{:S(2)}) async-start(), calls=%async_computation.26 | async-start | bytes 983040
  473.7 56.6 %reduce-scatter.17.cloned.1.call-start = ((), (), s32[]{:S(2)}) async-start(), calls=%async_computation.19 | async-start | bytes 1310720 | tf_op jit(solution)/shard_map/reduce_scatter | solution.py:308
  481.3 74.8 %reduce-scatter.19.cloned.1.call-start = ((), (), s32[]{:S(2)}) async-start(), calls=%async_computation.20 | async-start | bytes 1310720 | tf_op jit(solution)/shard_map/reduce_scatter | solution.py:311
  487.6 94.3 %reduce-scatter.15.cloned.1.call-start = ((), (), s32[]{:S(2)}) async-start(), calls=%async_computation.18 | async-start | bytes 1310720 | tf_op jit(solution)/shard_map/reduce_scatter | solution.py:305
  494.1 11.5 %copy-start.24 = (f32[192,32]{0,1:T(8,128)S(1)}, f32[192,32]{0,1:T(8,128)}, u32[]{:S(2)}) copy-start(f32[192,32]{0,1:T(8,128)} %copy-done.23) | copy-start | bytes 73732
  494.1 11.5 %copy-start.26 = (f32[192,32]{0,1:T(8,128)S(1)}, f32[192,32]{0,1:T(8,128)}, u32[]{:S(2)}) copy-start(f32[192,32]{0,1:T(8,128)} %copy-done.25) | copy-start | bytes 73732
  494.2 13.2 %copy-start.20 = (bf16[8,64,2,192]{3,1,2,0:T(8,128)(2,1)S(1)}, bf16[8,64,2,192]{3,1,2,0:T(8,128)(2,1)}, u32[]{:S(2)}) copy-start(bf16[8,64,2,192]{3,1,2,0:T(8,128)(2,1)} %fusion.48) | copy-start | bytes 1179652
  494.2 113.9 %reduce-scatter.25.cloned.1.call-start = ((), (), s32[]{:S(2)}) async-start(), calls=%async_computation.23 | async-start | bytes 1310720 | tf_op jit(solution)/shard_map/reduce_scatter | solution.py:288
  496.8 137.6 %reduce-scatter.23.cloned.1.call-start = ((), (), s32[]{:S(2)}) async-start(), calls=%async_computation.22 | async-start | bytes 1310720 | tf_op jit(solution)/shard_map/reduce_scatter | solution.py:285
  507.4 159.0 %reduce-scatter.27.cloned.1.call-start = ((), (), s32[]{:S(2)}) async-start(), calls=%async_computation.24 | async-start | bytes 2621440 | tf_op jit(solution)/shard_map/reduce_scatter | solution.py:291
  509.5 188.7 %reduce-scatter.21.cloned.1.call-start = ((), (), s32[]{:S(2)}) async-start(), calls=%async_computation.21 | async-start | bytes 2621440 | tf_op jit(solution)/shard_map/reduce_scatter | solution.py:282
  516.0 71.1 %copy-start.8 = (bf16[1024,512]{1,0:T(8,128)(2,1)S(1)}, bf16[1024,512]{1,0:T(8,128)(2,1)}, u32[]{:S(2)}) copy-start(bf16[1024,512]{1,0:T(8,128)(2,1)} %all-gather.9.cloned.1.call-done) | copy-start | bytes 3145732
  516.0 71.1 %copy-start.19 = (bf16[192,8,64]{0,2,1:T(8,128)(2,1)S(1)}, bf16[192,8,64]{0,2,1:T(8,128)(2,1)}, u32[]{:S(2)}) copy-start(bf16[192,8,64]{0,2,1:T(8,128)(2,1)} %copy-done.18) | copy-start | bytes 589828
  516.0 205.2 %reduce-scatter.29.cloned.1.call-start = ((), (), s32[]{:S(2)}) async-start(), calls=%async_computation.25 | async-start | bytes 81920 | tf_op jit(solution)/shard_map/reduce_scatter | solution.py:294
  584.6 113.7 %copy-start.33 = (bf16[192,512]{1,0:T(8,128)(2,1)S(1)}, bf16[192,512]{1,0:T(8,128)(2,1)}, u32[]{:S(2)}) copy-start(bf16[192,512]{1,0:T(8,128)(2,1)} %reduce-scatter.33.cloned.1.call-done) | copy-start | bytes 589828
  584.6 265.5 %all-reduce.12.cloned.1.call-start = ((), (), s32[]{:S(2)}) async-start(), calls=%async_computation.28 | async-start | bytes 3145728 | tf_op jit(solution)/shard_map/psum | solution.py:273
  587.1 261.8 %copy-start.52 = (f32[192]{0:T(256)S(1)}, f32[192]{0:T(256)}, u32[]{:S(2)}) copy-start(f32[192]{0:T(256)} %copy-done.51) | copy-start | bytes 2308
  698.3 159.6 %copy-start.1 = (bf16[1,1024,512]{2,1,0:T(8,128)(2,1)S(1)}, bf16[1,1024,512]{2,1,0:T(8,128)(2,1)}, u32[]{:S(2)}) copy-start(bf16[1,1024,512]{2,1,0:T(8,128)(2,1)} %param.25) | copy-start | bytes 3145732
  (33 other events, 146.6 us)
Sparse Core Ops, SparseCore 0:
  9.7 26.6 all-gather.6
  38.1 24.6 all-gather.8
  64.4 42.6 all-gather.10
  108.6 31.1 all-gather.12
  457.4 21.9 reduce-scatter.32
  482.2 22.2 reduce-scatter.30
  506.9 23.2 reduce-scatter.16
  532.8 23.2 reduce-scatter.18
  558.5 23.2 reduce-scatter.14
  584.8 23.2 reduce-scatter.24
  611.1 23.2 reduce-scatter.22
  636.8 29.4 reduce-scatter.26
  668.7 29.4 reduce-scatter.20
  701.2 20.0 reduce-scatter.28
  724.7 105.9 all-reduce.11
where the time goes:
time: 870 us; the launch traced here: 865 us
  waiting for transfers between devices  365 us (42%)
  blocking collectives  211 us (24%)
  matrix products  117 us (13%)
  local copies, waits for them, and re-layouts  76.2 us (9%)
  other arithmetic  49.8 us (6%)
  starting transfers between devices  28.7 us (3%)
  between operations  16.9 us (2%)
    psum x1, blocking collectives, local(): lax.psum(router_grad.astype(jnp.bfloat16), 'expert').astype(jnp.float32)  126 us
    all_to_all x1, waiting for transfers between devices, local(): lax.all_to_all(send_rows.reshape(send_shape), 'expert', split_axis=0, con...  46.5 us
    all_to_all x1, waiting for transfers between devices, local(): lax.all_to_all(expert_out.reshape(send_shape), 'expert', split_axis=0, co...  43.2 us
    all_to_all x1, waiting for transfers between devices, local(): lax.all_to_all(send_grad.reshape(send_shape), 'expert', split_axis=0, con...  42.5 us
    reduce_scatter x1, waiting for transfers between devices, local(): lax.psum_scatter(summed[0].astype(jnp.bfloat16), 'wshard', scatter_dimens...  31.9 us
    reduce_scatter x1, waiting for transfers between devices, local(): lax.psum_scatter(summed[3].astype(jnp.bfloat16), 'wshard', scatter_dimens...  31.9 us
    all_to_all x1, waiting for transfers between devices, local(): lax.all_to_all(row_grad.reshape(send_shape), 'expert', split_axis=0, conc...  27.3 us
    reduce_scatter x1, waiting for transfers between devices, local(): lax.psum_scatter(summed[1].astype(jnp.bfloat16), 'wshard', scatter_dimens...  26.3 us
  transfers between devices with their start and end apart: 19, of which 14 were waited for; matrix products, arithmetic and copies ran while one was open for 18% of the time, Pallas kernels for 0%

commit v1 on v0

v1 whole, which is shorter than its diff:
```python
import functools

import jax
import jax.numpy as jnp
from jax import lax
from jax.experimental import pallas as pl
from jax.experimental.pallas import tpu as pltpu
from jax.sharding import PartitionSpec as P

f32 = jnp.float32
bf16 = jnp.bfloat16
epsilon = 1e-06
residual_scale = 0.22
score_scale = 0.015625
rope_base = 10000.0

LANES = 4
OWNERS = 32
ROWS = 192
GROUP = 768
WIDTH = 1024
CAP = 64
SLOTS = OWNERS * CAP
FF = 512
TOP = 8
EXTRA = 128
VMEM = 50 * 1024 * 1024


def nn(a, b):
    return lax.dot_general(a, b, (((1,), (0,)), ((), ())), preferred_element_type=f32)


def nt(a, b):
    return lax.dot_general(a, b, (((1,), (1,)), ((), ())), preferred_element_type=f32)


def tn(a, b):
    return lax.dot_general(a, b, (((0,), (0,)), ((), ())), preferred_element_type=f32)


def iota(shape, axis):
    return lax.broadcasted_iota(jnp.int32, shape, axis)


def split_two(v):
    high = v.astype(bf16)
    return high, (v - high.astype(f32)).astype(bf16)


def call(kernel, name, outs, args, smem=0, scratch=()):
    specs = [pl.BlockSpec(memory_space=pltpu.SMEM)] * smem
    specs += [pl.BlockSpec(memory_space=pltpu.VMEM)] * (len(args) - smem)
    return pl.pallas_call(
        kernel,
        name=name,
        out_shape=[jax.ShapeDtypeStruct(s, d) for s, d in outs],
        in_specs=specs,
        out_specs=[pl.BlockSpec(memory_space=pltpu.VMEM)] * len(outs),
        scratch_shapes=list(scratch),
        compiler_params=pltpu.CompilerParams(vmem_limit_bytes=VMEM),
    )(*args)


def routing_kernel(routes, routes_t, cot, pick, pick_t, mask_out, rows_out):
    lane = iota((ROWS, EXTRA), 1)
    mask = jnp.zeros((ROWS, EXTRA), f32)
    for k in range(TOP):
        mask += (routes[:, k : k + 1] == lane).astype(f32)
    sub = iota((OWNERS, ROWS), 0)
    mask_t = jnp.zeros((OWNERS, ROWS), f32)
    for k in range(TOP):
        mask_t += (routes_t[k : k + 1, :] == sub).astype(f32)
    mask_b = mask.astype(bf16)
    mask_tb = mask_t.astype(bf16)
    i0, i1 = iota((ROWS, ROWS), 0), iota((ROWS, ROWS), 1)
    before = nn((i1 < i0).astype(f32).astype(bf16), mask_b).astype(bf16)
    before_t = nn(mask_tb, (i0 < i1).astype(f32).astype(bf16)).astype(bf16)
    spread = ((iota((EXTRA, SLOTS), 1) // CAP) == iota((EXTRA, SLOTS), 0)).astype(f32).astype(bf16)
    spread_t = ((iota((SLOTS, OWNERS), 0) // CAP) == iota((SLOTS, OWNERS), 1)).astype(f32)
    spread_t = spread_t.astype(bf16)
    slot = (iota((ROWS, SLOTS), 1) % CAP).astype(f32)
    slot_t = (iota((SLOTS, ROWS), 0) % CAP).astype(f32)
    p = jnp.where(nn(before, spread) == slot, nn(mask_b, spread), 0.0)
    p_t = jnp.where(nn(spread_t, before_t) == slot_t, nn(spread_t, mask_tb), 0.0)
    pick[...] = p.astype(bf16)
    pick_t[...] = p_t.astype(bf16)
    mask_out[...] = mask
    p_tb = p_t.astype(bf16)
    rows_out[:, :WIDTH] = nn(p_tb, cot[...]).astype(bf16)
    rows_out[:, WIDTH:] = nn(p_tb, mask_b).astype(bf16)


def swap_halves(t):
    lane = iota(t.shape, 1) % 64
    return jnp.where(lane < 32, pltpu.roll(t, 96, 1), pltpu.roll(t, 32, 1))


def allowed(split, low, rows, keys):
    qi = iota((rows, keys), 0) + low
    kj = iota((rows, keys), 1)
    start = jnp.where(qi >= split, split, 0)
    return (kj <= qi) & (kj >= start)


BLOCK = 256
BLOCKS = GROUP // BLOCK


def head_place(h):
    return h // 2, h % 2, (h // 2) != (h % 2)


def front_kernel(split, x_ref, w_ref, gain, cosine, sine, normed, q_out, k_out, v_out, mixed):
    x = x_ref[...].astype(f32)
    factor = lax.rsqrt(jnp.mean(x * x, axis=-1, keepdims=True) + epsilon)
    normed_b = (x * factor * gain[...]).astype(bf16)
    normed[...] = normed_b
    lin = nn(normed_b, w_ref[:, :512])
    c, s = cosine[...], sine[...]
    for g in range(2):
        part = lin[:, 128 * g : 128 * g + 128]
        q_out[:, 128 * g : 128 * g + 128] = (part * c + swap_halves(part) * s).astype(bf16)
    part = lin[:, 256:384]
    key = part * c + swap_halves(part) * s
    key_b = key.astype(bf16)
    k_out[...] = key_b
    value_b = lin[:, 384:512].astype(bf16)
    v_out[...] = value_b
    keys = (key_b, pltpu.roll(key_b.astype(f32), 64, 1).astype(bf16))
    values = (value_b, pltpu.roll(value_b.astype(f32), 64, 1).astype(bf16))
    low_half = iota((BLOCK, 128), 1) < 64
    for i in range(BLOCKS):
        n = (i + 1) * BLOCK
        ok = allowed(split[0], i * BLOCK, BLOCK, n)
        for g in range(2):
            q2 = q_out[i * BLOCK : (i + 1) * BLOCK, 128 * g : 128 * g + 128].astype(f32) * score_scale
            halves = []
            for half in range(2):
                turned = g != half
                mine = low_half if half == 0 else ~low_half
                qh = jnp.where(mine, q2, 0.0).astype(bf16)
                scores = jnp.where(ok, nt(qh, keys[turned][:n]), -1e30)
                top = jnp.max(scores, axis=-1, keepdims=True)
                e = jnp.exp(scores - top)
                probs = (e / jnp.sum(e, axis=-1, keepdims=True)).astype(bf16)
                halves.append(nn(probs, values[turned][:n]))
            mixed[i * BLOCK : (i + 1) * BLOCK, 128 * g : 128 * g + 128] = jnp.where(
                low_half, halves[0], halves[1]
            ).astype(bf16)


def middle_kernel(mixed, w_out, x_ref, gain, router, mask, pick_t, middle, second, gate, rows_out):
    mid = x_ref[...].astype(f32) + residual_scale * nn(mixed[...], w_out[...])
    middle[...] = mid
    factor = lax.rsqrt(jnp.mean(mid * mid, axis=-1, keepdims=True) + epsilon)
    second_b = (mid * factor * gain[...]).astype(bf16)
    second[...] = second_b
    chosen = mask[...] > 0.5
    logits = jnp.where(chosen, nn(second_b, router[...]), -1e30)
    top = jnp.max(logits, axis=-1, keepdims=True)
    e = jnp.where(chosen, jnp.exp(logits - top), 0.0)
    gate[...] = e / jnp.sum(e, axis=-1, keepdims=True)
    rows_out[...] = nn(pick_t[...], second_b).astype(bf16)


EXPERT_BLOCK = 256


def expert_kernel(
    me, rows, h_up, mask, router, w_gate, w_up, g_rows, hidden, g_gate, g_up, gate_out
):
    r = rows[...]
    lane = iota((EXPERT_BLOCK, EXTRA), 1)
    chosen = mask[...].astype(f32) > 0.5
    logits = jnp.where(chosen, nn(r, router[...]), -1e30)
    top = jnp.max(logits, axis=-1, keepdims=True)
    e = jnp.where(chosen, jnp.exp(logits - top), 0.0)
    total = jnp.sum(e, axis=-1, keepdims=True)
    mine = jnp.sum(jnp.where(lane == me[0], e, 0.0), axis=-1, keepdims=True)
    gate = mine / jnp.where(total > 0, total, 1.0)
    gate_out[...] = jnp.broadcast_to(gate, (EXPERT_BLOCK, EXTRA))
    gate_lin = nn(r, w_gate[...])
    up_lin = nn(r, w_up[...])
    sig = 1.0 / (1.0 + jnp.exp(-gate_lin))
    act = gate_lin * sig
    hidden_b = (act * up_lin).astype(bf16)
    hidden[...] = hidden_b
    up = h_up[...].astype(f32)
    g = residual_scale * jnp.sum(hidden_b.astype(f32) * up, axis=-1, keepdims=True)
    g_hidden = ((residual_scale * gate) * up).astype(bf16).astype(f32)
    gg = (g_hidden * up_lin * (sig * (1.0 + gate_lin * (1.0 - sig)))).astype(bf16)
    gu = (g_hidden * act).astype(bf16)
    g_gate[...] = gg
    g_up[...] = gu
    g_rows[:, :WIDTH] = (nt(gg, w_gate[...]) + nt(gu, w_up[...])).astype(bf16)
    high = g.astype(bf16).astype(f32)
    g_rows[:, WIDTH:] = jnp.where(
        lane == me[0], high, jnp.where(lane == me[0] + OWNERS, g - high, 0.0)
    ).astype(bf16)


def expert_call(me, rows, h_up, ups, router, w_gate, w_up):
    def whole(shape):
        return pl.BlockSpec(shape, lambda i: (0, 0))

    def blocked(width, column=0):
        return pl.BlockSpec((EXPERT_BLOCK, width), lambda i: (i, column))

    return pl.pallas_call(
        expert_kernel,
        name="expert",
        grid=(SLOTS // EXPERT_BLOCK,),
        out_shape=[
            jax.ShapeDtypeStruct((SLOTS, WIDTH + EXTRA), bf16),
            jax.ShapeDtypeStruct((SLOTS, FF), bf16),
            jax.ShapeDtypeStruct((SLOTS, FF), bf16),
            jax.ShapeDtypeStruct((SLOTS, FF), bf16),
            jax.ShapeDtypeStruct((SLOTS, EXTRA), f32),
        ],
        in_specs=[
            pl.BlockSpec(memory_space=pltpu.SMEM),
            blocked(WIDTH),
            blocked(FF),
            blocked(EXTRA, WIDTH // EXTRA),
            whole((WIDTH, EXTRA)),
            whole((WIDTH, FF)),
            whole((WIDTH, FF)),
        ],
        out_specs=[blocked(WIDTH + EXTRA), blocked(FF), blocked(FF), blocked(FF), blocked(EXTRA)],
        compiler_params=pltpu.CompilerParams(vmem_limit_bytes=VMEM),
    )(me, rows, h_up, ups, router, w_gate, w_up)


def return_kernel(
    back, pick, middle, second, gate, cot, router, gain, g_middle_out, g_branch, small_out
):
    ext = nn(pick[...], back[...])
    lane = iota((ROWS, EXTRA), 1)
    tail = ext[:, WIDTH:]
    g_gate = jnp.where(lane < OWNERS, tail + pltpu.roll(tail, EXTRA - OWNERS, 1), 0.0)
    probs = gate[...]
    g_logits = probs * (g_gate - jnp.sum(probs * g_gate, axis=-1, keepdims=True))
    high, low = split_two(g_logits)
    w = router[...]
    g_second = ext[:, :WIDTH] + (nt(high, w) + nt(low, w))
    mid = middle[...]
    factor = lax.rsqrt(jnp.mean(mid * mid, axis=-1, keepdims=True) + epsilon)
    z = mid * factor
    t = g_second * gain[...]
    g_middle = cot[...].astype(f32) + factor * (t - z * jnp.mean(t * z, axis=-1, keepdims=True))
    g_middle_out[...] = g_middle
    g_branch[...] = (residual_scale * g_middle).astype(bf16)
    s = second[...]
    one = (lane == OWNERS).astype(f32).astype(bf16)
    ph, plow = split_two(g_second * z)
    small_out[...] = tn(s, high) + tn(s, low) + tn(ph, one) + tn(plow, one)


def back_kernel(
    split,
    gb,
    gb_cols,
    w_out,
    mixed_all,
    q_ref,
    k_ref,
    v_ref,
    normed,
    x_ref,
    w_ref,
    cosine,
    sine,
    small_in,
    grads,
    g_normed_out,
    g_mixed,
    g_query,
    g_key,
    g_value,
):
    g_mixed[...] = nt(gb[...], w_out[...]).astype(bf16)
    key_b, value_b = k_ref[...], v_ref[...]
    keys = (key_b, pltpu.roll(key_b.astype(f32), 64, 1).astype(bf16))
    values = (value_b, pltpu.roll(value_b.astype(f32), 64, 1).astype(bf16))
    g_key[...] = jnp.zeros_like(g_key)
    g_value[...] = jnp.zeros_like(g_value)
    low_half = iota((BLOCK, 128), 1) < 64
    for i in range(BLOCKS):
        n = (i + 1) * BLOCK
        here = slice(i * BLOCK, (i + 1) * BLOCK)
        ok = allowed(split[0], i * BLOCK, BLOCK, n)
        for g in range(2):
            q2 = q_ref[here, 128 * g : 128 * g + 128].astype(f32) * score_scale
            gm2 = g_mixed[here, 128 * g : 128 * g + 128].astype(f32)
            halves = []
            for half in range(2):
                turned = int(g != half)
                mine = low_half if half == 0 else ~low_half
                qh = jnp.where(mine, q2, 0.0).astype(bf16)
                gm = jnp.where(mine, gm2, 0.0).astype(bf16)
                scores = jnp.where(ok, nt(qh, keys[turned][:n]), -1e30)
                top = jnp.max(scores, axis=-1, keepdims=True)
                e = jnp.exp(scores - top)
                probs = e / jnp.sum(e, axis=-1, keepdims=True)
                gp = nt(gm, values[turned][:n])
                pg = probs * gp
                gs = (pg - probs * jnp.sum(pg, axis=-1, keepdims=True)).astype(bf16)
                halves.append(nn(gs, keys[turned][:n]))
                g_key[turned, :n, :] += tn(gs, qh)
                g_value[turned, :n, :] += tn(probs.astype(bf16), gm)
            g_query[here, 128 * g : 128 * g + 128] = score_scale * jnp.where(
                low_half, halves[0], halves[1]
            )
    c, s = cosine[...], sine[...]

    def unturn(t):
        return (t * c - swap_halves(t) * s).astype(bf16)

    g_lin = jnp.concatenate(
        [
            unturn(g_query[:, :128]),
            unturn(g_query[:, 128:]),
            unturn(g_key[0] + pltpu.roll(g_key[1], 64, 1)),
            (g_value[0] + pltpu.roll(g_value[1], 64, 1)).astype(bf16),
        ],
        axis=1,
    )
    grads[:, :512] = tn(normed[...], g_lin).astype(bf16)
    grads[:, 512:768] = tn(mixed_all[...], gb_cols[...]).astype(bf16)
    g_normed = nt(g_lin, w_ref[:, :512])
    g_normed_out[...] = g_normed.astype(bf16)
    x = x_ref[...].astype(f32)
    y = x * lax.rsqrt(jnp.mean(x * x, axis=-1, keepdims=True) + epsilon)
    one = (iota((GROUP, EXTRA), 1) == OWNERS + 1).astype(f32).astype(bf16)
    ph, plow = split_two(g_normed * y)
    grads[:, 768:] = (small_in[...] + tn(ph, one) + tn(plow, one)).astype(bf16)


def z_shift(value, d):
    return lax.ppermute(value, "wshard", [(i, (i + d) % LANES) for i in range(LANES)])


def by_source(pieces, z, axis=0):
    stacked = jnp.stack(pieces)
    return jnp.concatenate(
        [
            lax.dynamic_index_in_dim(stacked, (z - a) % LANES, 0, keepdims=False)
            for a in range(LANES)
        ],
        axis=axis,
    )


def gather_z(value, z, axis=0):
    return by_source([value] + [z_shift(value, d) for d in (1, 2, 3)], z, axis)


def both_cores(value, core):
    other = lax.ppermute(value, "expert", [(i, i ^ 1) for i in range(OWNERS)])
    first = jnp.where(core == 0, value, other)
    last = jnp.where(core == 0, other, value)
    return first, last


def to_owners(value):
    return lax.all_to_all(value, "expert", 0, 0, tiled=True)


def local(
    tokens,
    w_query,
    w_key,
    w_value,
    w_out,
    w_router,
    gain_attn,
    gain_moe,
    w_gate,
    w_up,
    w_down,
    routes,
    seq_split,
    cotangent,
):
    z = lax.axis_index("wshard")
    me = lax.axis_index("expert")
    core = me % 2
    w_gate, w_up, w_down = w_gate[0], w_up[0], w_down[0]

    pick, pick_t, mask, ups_send = call(
        routing_kernel,
        "routing",
        [
            ((ROWS, SLOTS), bf16),
            ((SLOTS, ROWS), bf16),
            ((ROWS, EXTRA), f32),
            ((SLOTS, WIDTH + EXTRA), bf16),
        ],
        (routes, routes.T, cotangent),
    )
    ups = to_owners(ups_send.reshape(OWNERS, CAP, WIDTH + EXTRA)).reshape(SLOTS, WIDTH + EXTRA)

    x_all = gather_z(tokens, z)
    small = jnp.concatenate(
        [
            w_router,
            gain_attn[:, None],
            gain_moe[:, None],
            jnp.zeros((256, EXTRA - OWNERS - 2), bf16),
        ],
        axis=1,
    )

    def columns_for(dest):
        row = core * 128
        return jnp.concatenate(
            [
                lax.dynamic_slice(w_query, (row, dest * 256), (128, 256)),
                lax.dynamic_slice(w_key, (row, dest * 128), (128, 128)),
                lax.dynamic_slice(w_value, (row, dest * 128), (128, 128)),
                lax.dynamic_slice(small, (row, 0), (128, EXTRA)),
            ],
            axis=1,
        )

    pieces = [columns_for(z)] + [z_shift(columns_for((z + d) % LANES), d) for d in (1, 2, 3)]
    mine = by_source(pieces, z).reshape(LANES, 128, 640)
    first, last = both_cores(mine, core)
    w_all = jnp.stack([first, last], axis=1).reshape(WIDTH, 640)
    small_all = w_all[:, 512:]
    gain_a = small_all[:, OWNERS].astype(f32)[None, :]
    gain_m = small_all[:, OWNERS + 1].astype(f32)[None, :]

    half_out = lax.dynamic_slice(w_out, (core * 128, 0), (128, WIDTH))
    out_mine = gather_z(half_out, z).reshape(LANES, 128, WIDTH)
    first, last = both_cores(out_mine, core)
    out_all = jnp.stack([first, last], axis=1).reshape(WIDTH, WIDTH)

    split_at = seq_split[0]
    places = jnp.arange(GROUP, dtype=jnp.int32)
    position = jnp.where(places >= split_at, places - split_at, places).astype(f32)
    exponent = jnp.arange(32, dtype=f32) * (2.0 / 64)
    angles = position[:, None] * jnp.power(rope_base, -exponent)[None, :]
    cosine, sine = jnp.cos(angles), jnp.sin(angles)
    cosine = jnp.concatenate([cosine] * 4, axis=1)
    sine = jnp.concatenate([-sine, sine] * 2, axis=1)

    normed, query, key, value, mixed = call(
        front_kernel,
        "attention",
        [
            ((GROUP, WIDTH), bf16),
            ((GROUP, 256), bf16),
            ((GROUP, 128), bf16),
            ((GROUP, 128), bf16),
            ((GROUP, 256), bf16),
        ],
        (seq_split, x_all, w_all, gain_a, cosine, sine),
        smem=1,
    )
    by_row = mixed.reshape(LANES, ROWS, 256)

    def rows_for(dest):
        return lax.dynamic_index_in_dim(by_row, dest, 0, keepdims=False)

    mixed_own = by_source(
        [rows_for(z)] + [z_shift(rows_for((z + d) % LANES), d) for d in (1, 2, 3)], z, 1
    )
    middle, second, gate, rows_send = call(
        middle_kernel,
        "middle",
        [
            ((ROWS, WIDTH), f32),
            ((ROWS, WIDTH), bf16),
            ((ROWS, EXTRA), f32),
            ((SLOTS, WIDTH), bf16),
        ],
        (mixed_own, out_all, tokens, gain_m, small_all, mask, pick_t),
    )
    rows_in = to_owners(rows_send.reshape(OWNERS, CAP, WIDTH)).reshape(SLOTS, WIDTH)
    mixed_all = gather_z(mixed, z, 1)

    up_rows = ups[:, :WIDTH]
    h_up = nt(up_rows, w_down).astype(bf16)
    g_rows, hidden, g_gate, g_up, gate_rows = expert_call(
        me.reshape(1), rows_in, h_up, ups, small_all, w_gate, w_up
    )
    back = to_owners(g_rows.reshape(OWNERS, CAP, WIDTH + EXTRA)).reshape(SLOTS, WIDTH + EXTRA)

    row_gate = gate_rows[:, :1]
    expert_out = nn(hidden, w_down).astype(bf16).astype(f32)
    out_back = to_owners((row_gate * expert_out).astype(bf16).reshape(OWNERS, CAP, WIDTH))
    g_out = (residual_scale * row_gate * up_rows.astype(f32)).astype(bf16)
    gate_grad = tn(rows_in, g_gate).astype(bf16)
    up_grad = tn(rows_in, g_up).astype(bf16)
    down_grad = tn(hidden, g_out).astype(bf16)
    packed = jnp.concatenate(
        [
            gate_grad.reshape(LANES, 256, FF),
            up_grad.reshape(LANES, 256, FF),
            down_grad[:, :FF].reshape(LANES, 128, FF),
            down_grad[:, FF:].reshape(LANES, 128, FF),
        ],
        axis=1,
    )

    def part_for(dest):
        return lax.dynamic_index_in_dim(packed, dest, 0, keepdims=False)

    expert_sum = part_for(z).astype(f32)
    for d in (1, 2, 3):
        expert_sum += z_shift(part_for((z + d) % LANES), d).astype(f32)
    gate_share = expert_sum[None, :256]
    up_share = expert_sum[None, 256:512]
    down_share = jnp.concatenate([expert_sum[512:640], expert_sum[640:]], axis=1)[None]

    g_middle, g_branch, small_grad = call(
        return_kernel,
        "return",
        [((ROWS, WIDTH), f32), ((ROWS, WIDTH), bf16), ((WIDTH, EXTRA), f32)],
        (back, pick, middle, second, gate, cotangent, small_all, gain_m),
    )
    branch_all = gather_z(g_branch, z)
    branch_cols = lax.dynamic_slice(branch_all, (0, z * 256), (GROUP, 256))
    grads, g_normed = call(
        back_kernel,
        "attention_back",
        [((WIDTH, 768 + EXTRA), bf16), ((GROUP, WIDTH), bf16)],
        (
            seq_split,
            branch_all,
            branch_cols,
            w_out,
            mixed_all,
            query,
            key,
            value,
            normed,
            x_all,
            w_all,
            cosine,
            sine,
            small_grad,
        ),
        smem=1,
        scratch=[
            pltpu.VMEM((GROUP, 256), bf16),
            pltpu.VMEM((GROUP, 256), f32),
            pltpu.VMEM((2, GROUP, 128), f32),
            pltpu.VMEM((2, GROUP, 128), f32),
        ],
    )

    wide = 768 + EXTRA
    spread = grads.reshape(LANES, OWNERS, 8, wide).transpose(1, 0, 2, 3).reshape(128, 8, wide)
    arrived = lax.all_to_all(spread, ("expert", "wshard"), 0, 0, tiled=True)
    summed = jnp.sum(arrived.reshape(OWNERS, LANES, 8, wide).astype(f32), axis=0)
    small_sum = jnp.sum(summed[:, :, 768:], axis=0)
    strip = jnp.concatenate(
        [summed[a, :, :256] for a in range(LANES)]
        + [summed[a, :, 256:384] for a in range(LANES)]
        + [summed[a, :, 384:512] for a in range(LANES)]
        + [summed[a, :, 512:768] for a in range(LANES)]
        + [small_sum],
        axis=1,
    ).astype(bf16)
    shared = to_owners(jnp.broadcast_to(strip[None], (OWNERS,) + strip.shape))
    shared = shared.reshape(256, strip.shape[1]).astype(f32)

    output = middle + residual_scale * nn(pick, out_back.reshape(SLOTS, WIDTH))

    by_group = g_normed.reshape(LANES, ROWS, WIDTH)

    def normed_for(dest):
        return lax.dynamic_index_in_dim(by_group, dest, 0, keepdims=False)

    g_own = normed_for(z).astype(f32)
    for d in (1, 2, 3):
        g_own += z_shift(normed_for((z + d) % LANES), d).astype(f32)
    x = tokens.astype(f32)
    factor = lax.rsqrt(jnp.mean(x * x, axis=-1, keepdims=True) + epsilon)
    y = x * factor
    t = g_own * gain_a
    input_grad = g_middle + factor * (t - y * jnp.mean(t * y, axis=-1, keepdims=True))

    return (
        output,
        input_grad,
        shared[:, :1024],
        shared[:, 1024:1536],
        shared[:, 1536:2048],
        shared[:, 2048:3072],
        shared[:, 3072 : 3072 + OWNERS],
        shared[:, 3072 + OWNERS + 1],
        shared[:, 3072 + OWNERS],
        gate_share,
        up_share,
        down_share,
    )


def solution(mesh):
    rows = P(("expert", "wshard"), None)
    dense = P("wshard", None)
    expert = P("expert", None, None)
    shard = P("expert", "wshard", None)
    in_specs = (rows,) + (dense,) * 5 + (P("wshard"),) * 2 + (expert,) * 3
    in_specs += (rows, P("expert"), rows)
    out_specs = (rows, rows) + (dense,) * 5 + (P("wshard"),) * 2 + (shard,) * 3
    return jax.shard_map(local, mesh=mesh, in_specs=in_specs, out_specs=out_specs, check_vma=False)
```

time: 870 us -> 466 us (0.54)
  blocking collectives: 211 us -> 0 us
  waiting for transfers between devices: 365 us -> 237 us
  matrix products: 117 us -> 31.5 us
  Pallas kernels: 0 us -> 57.9 us
  starting transfers between devices: 28.7 us -> 78.4 us
  local copies, waits for them, and re-layouts: 76.2 us -> 30.2 us
  other arithmetic: 49.8 us -> 19.9 us
  between operations: 16.9 us -> 2.5 us
    reduce_scatter x8 -> x0, waiting for transfers between devices: 183 us -> none  [the longest x1 31.9 us: local(): lax.psum_scatter(summed[0].astype(jnp.bfloat16), 'wshard', scatter_dimens...]
    psum x1 -> x0, blocking collectives: 126 us -> none  [local(): lax.psum(router_grad.astype(jnp.bfloat16), 'expert').astype(jnp.float32)]
    ppermute x0 -> x26, waiting for transfers between devices: none -> 118 us  [the longest x24 118 us: z_shift(): lax.ppermute(value, 'wshard', [(i, (i + d) % LANES) for i in range(LANES)])]
    dot_general x32 -> x6, matrix products: 117 us -> 31.5 us  [the longest x3 17.1 us: tn(): lax.dot_general(a, b, (((0,), (0,)), ((), ())), preferred_element_type=f32)]
    all_gather x5 -> x0, blocking collectives: 76.5 us -> none  [the longest x1 25.2 us: local(): lax.all_gather(value_b, 'wshard', axis=0, tiled=True)]
    pallas_call x0 -> x6, Pallas kernels: none -> 57.9 us  [the longest x5 42.9 us: call(): pl.pallas_call(kernel, name=name, out_shape=[jax.ShapeDtypeStruct(s, d) f...]
    gather x10 -> x0, local copies, waits for them, and re-layouts: 46.5 us -> none  [the longest x5 14.6 us: local(): chosen = jnp.take_along_axis(logits, routes, axis=1)]
    all_to_all x4 -> x6, waiting for transfers between devices: 159 us -> 120 us  [the longest x5 120 us: to_owners(): return lax.all_to_all(value, 'expert', 0, 0, tiled=True)]
  transfers between devices with their start and end apart: 19 -> 32, of which waited for: 14 -> 21; matrix products, arithmetic and copies ran while one was open for 18% -> 12% of each run, Pallas kernels for 0% -> 3%
where the time goes in v1:
time: 466 us; the launch traced here: 457 us
  waiting for transfers between devices  237 us (51%)
  starting transfers between devices  78.4 us (17%)
  Pallas kernels  57.9 us (12%)
  matrix products  31.5 us (7%)
  local copies, waits for them, and re-layouts  30.2 us (6%)
  other arithmetic  19.9 us (4%)
    all_to_all x5, waiting for transfers between devices, to_owners(): return lax.all_to_all(value, 'expert', 0, 0, tiled=True)  120 us
    ppermute x24, waiting for transfers between devices, z_shift(): lax.ppermute(value, 'wshard', [(i, (i + d) % LANES) for i in range(LANES)])  118 us
    pallas_call x5, Pallas kernels, call(): pl.pallas_call(kernel, name=name, out_shape=[jax.ShapeDtypeStruct(s, d) f...  42.9 us
    all_to_all x5, starting transfers between devices, to_owners(): return lax.all_to_all(value, 'expert', 0, 0, tiled=True)  35.3 us
    ppermute x24, starting transfers between devices, z_shift(): lax.ppermute(value, 'wshard', [(i, (i + d) % LANES) for i in range(LANES)])  32.9 us
    dot_general x3, matrix products, tn(): lax.dot_general(a, b, (((0,), (0,)), ((), ())), preferred_element_type=f32)  17.1 us
    pallas_call x1, Pallas kernels, expert_call(): pl.pallas_call(expert_kernel, name='expert', grid=(SLOTS // EXPERT_BLOCK,...  15 us
    unnamed x113, local copies, waits for them, and re-layouts  14.8 us
  transfers between devices with their start and end apart: 32, of which 21 were waited for; matrix products, arithmetic and copies ran while one was open for 12% of the time, Pallas kernels for 3%

profile of v1, /device:TPU:0, one launch (start us, length us, event | category | flops | bytes accessed | tf_op | source)
XLA Modules:
  0.0 457.5 jit_solution(11658580354915707889)
XLA Ops:
  3.3 5.4 %routing.1 = (bf16[192,2048]{1,0:T(8,128)(2,1)S(1)}, bf16[2048,192]{1,0:T(8,128)(2,1)S(1)}, f32[192,128]{1,0:T(8,128)S(1)}, bf16[2048,1152]{1,0:T(8,128)(2,1)}) custom-call(s32[192,8]{1,0:T(8,128)S(1)} %copy.56.routes, s32[8,192]{1,0:T(8,128)S(1)} %bitcast.244, bf16[192,1024]{1,0:T(8,128)(2,1)S(1)} %copy-done.11), custom_call_target="tpu_custom_call" | custom-call | tf_op jit(solution)/shard_map/routing/pallas_call | solution.py:54
  10.5 7.7 %all-to-all-start.1 = ((bf16[32,64,1152]{2,1,0:T(8,128)(2,1)}), bf16[32,64,1152]{2,1,0:T(8,128)(2,1)}, u32[]{:S(2)}, u32[]{:S(2)}) async-start(bf16[32,64,1152]{2,1,0:T(8,128)(2,1)} %bitcast.247), calls=%async_computation.1 | async-start | bytes 9437184 | tf_op jit(solution)/shard_map/all_to_all | solution.py:367
  18.9 1.9 collective-permute-start.10
  20.9 3.6 collective-permute-start.11
  26.0 2.1 collective-permute-start.5
  31.6 9.4 %collective-permute-done.4 = bf16[128,640]{1,0:T(8,128)(2,1)} collective-permute-done((bf16[128,640]{1,0:T(8,128)(2,1)}, bf16[128,640]{1,0:T(8,128)(2,1)}, u32[]{:S(2)}, u32[]{:S(2)}) %collective-permute-start.4) | collective-permute-done | bytes 163872 | tf_op jit(solution)/shard_map/ppermute | solution.py:341
  41.1 2.0 collective-permute-start
  45.6 1.7 collective-permute-start.2
  47.3 3.2 collective-permute-done.12
  52.8 7.8 %collective-permute-done.1 = bf16[192,1024]{1,0:T(8,128)(2,1)S(1)} collective-permute-done((bf16[192,1024]{1,0:T(8,128)(2,1)S(1)}, bf16[192,1024]{1,0:T(8,128)(2,1)S(1)}, u32[]{:S(2)}, u32[]{:S(2)}) %collective-permute-start.1) | collective-permute-done | bytes 393248 | tf_op jit(solution)/shard_map/ppermute | solution.py:341
  60.6 4.5 collective-permute-done.2
  67.3 8.5 %attention.1 = (bf16[768,1024]{1,0:T(8,128)(2,1)}, bf16[768,256]{1,0:T(8,128)(2,1)S(1)}, bf16[768,128]{1,0:T(8,128)(2,1)S(1)}, bf16[768,128]{1,0:T(8,128)(2,1)S(1)}, bf16[768,256]{1,0:T(8,128)(2,1)S(1)}) custom-call(s32[1]{0:T(128)} %copy.75.split, bf16[768,1024]{1,0:T(8,128)(2,1)} %pad_maximum_fusion.3.x_ref, bf16[1024,640]{1,0:T(8,128)(2,1)S(1)} %bitcast.232, ...), custom_call_target="tpu_custom_call" | custom-call | tf_op jit(solution)/shard_map/attention/pallas_call | solution.py:54
  76.6 2.9 collective-permute-start.8
  79.9 4.1 collective-permute-done.7
  86.2 5.7 %middle.1 = (f32[192,1024]{1,0:T(8,128)S(1)}, bf16[192,1024]{1,0:T(8,128)(2,1)S(1)}, f32[192,128]{1,0:T(8,128)S(1)}, bf16[2048,1024]{1,0:T(8,128)(2,1)}) custom-call(bf16[192,1024]{1,0:T(8,128)(2,1)S(1)} %pad_maximum_fusion.16.mixed, bf16[1024,1024]{1,0:T(8,128)(2,1)} %bitcast.245, bf16[192,1024]{1,0:T(8,128)(2,1)S(1)} %copy-done.2, ...), custom_call_target="tpu_custom_call" | custom-call | tf_op jit(solution)/shard_map/middle/pallas_call | solution.py:54
  93.5 7.7 %all-to-all-start = ((bf16[32,64,1024]{2,1,0:T(8,128)(2,1)}), bf16[32,64,1024]{2,1,0:T(8,128)(2,1)}, u32[]{:S(2)}, u32[]{:S(2)}) async-start(bf16[32,64,1024]{2,1,0:T(8,128)(2,1)} %bitcast.252), calls=%async_computation | async-start | bytes 8388608 | tf_op jit(solution)/shard_map/all_to_all | solution.py:367
  101.2 5.9 %fusion.5.h_up = bf16[2048,512]{1,0:T(8,128)(2,1)} fusion(bf16[2048,1152]{1,0:T(8,128)(2,1)} %bitcast.51.mask, bf16[1,512,1024]{2,1,0:T(8,128)(2,1)S(1)} %copy-done), kind=kOutput, calls=%fused_computation.9 | convolution fusion | flops 2148532224 | bytes 7340032 | tf_op jit(solution)/shard_map/dot_general | solution.py:35
  107.1 46.8 %all-to-all-done = bf16[32,64,1024]{2,1,0:T(8,128)(2,1)} async-done(((bf16[32,64,1024]{2,1,0:T(8,128)(2,1)}), bf16[32,64,1024]{2,1,0:T(8,128)(2,1)}, u32[]{:S(2)}, u32[]{:S(2)}) %all-to-all-start) | async-done | bytes 4194336 | tf_op jit(solution)/shard_map/all_to_all | solution.py:367
  156.4 15.0 %expert.1 = (bf16[2048,1152]{1,0:T(8,128)(2,1)}, bf16[2048,512]{1,0:T(8,128)(2,1)}, bf16[2048,512]{1,0:T(8,128)(2,1)}, bf16[2048,512]{1,0:T(8,128)(2,1)}, f32[2048,128]{1,0:T(8,128)S(1)}) custom-call(s32[1]{0:T(128)} %bitcast.47.me, bf16[2048,1024]{1,0:T(8,128)(2,1)} %bitcast.49.rows, bf16[2048,512]{1,0:T(8,128)(2,1)} %fusion.5.h_up, ...), custom_call_target="tpu_custom_call" | custom-call | tf_op jit(solution)/shard_map/expert/pallas_call | solution.py:210
  172.4 6.8 %all-to-all-start.3 = ((bf16[32,64,1152]{2,1,0:T(8,128)(2,1)}), bf16[32,64,1152]{2,1,0:T(8,128)(2,1)}, u32[]{:S(2)}, u32[]{:S(2)}) async-start(bf16[32,64,1152]{2,1,0:T(8,128)(2,1)} %bitcast.248), calls=%async_computation.3 | async-start | bytes 9437184 | tf_op jit(solution)/shard_map/all_to_all | solution.py:367
  180.2 2.9 collective-permute-start.18
  183.1 8.7 %collective-permute-done.17 = bf16[768,256]{1,0:T(8,128)(2,1)S(1)} collective-permute-done((bf16[768,256]{1,0:T(8,128)(2,1)S(1)}, bf16[768,256]{1,0:T(8,128)(2,1)S(1)}, u32[]{:S(2)}, u32[]{:S(2)}) %collective-permute-start.17) | collective-permute-done | bytes 393248 | tf_op jit(solution)/shard_map/ppermute | solution.py:341
  191.9 8.8 %collective-permute-done.18 = bf16[768,256]{1,0:T(8,128)(2,1)S(1)} collective-permute-done((bf16[768,256]{1,0:T(8,128)(2,1)S(1)}, bf16[768,256]{1,0:T(8,128)(2,1)S(1)}, u32[]{:S(2)}, u32[]{:S(2)}) %collective-permute-start.18) | collective-permute-done | bytes 393248 | tf_op jit(solution)/shard_map/ppermute | solution.py:341
  203.6 5.8 %convolution_convert_fusion.1 = bf16[1024,512]{1,0:T(8,128)(2,1)} fusion(bf16[2048,1024]{1,0:T(8,128)(2,1)} %bitcast.49.rows, bf16[2048,512]{1,0:T(8,128)(2,1)S(1)} %copy-done.46), kind=kOutput, calls=%fused_computation.23 | convolution fusion | flops 2148007936 | bytes 7340032 | tf_op jit(solution)/shard_map/dot_general | solution.py:39
  209.3 5.8 %fusion.10 = bf16[512,1024]{1,0:T(8,128)(2,1)} fusion(bf16[2048,512]{1,0:T(8,128)(2,1)S(1)} %copy-done.43, f32[2048]{0:T(1024)S(1)} %get-tuple-element.110, bf16[2048,1152]{1,0:T(8,128)(2,1)} %bitcast.51.mask), kind=kOutput, calls=%fused_computation.21 | convolution fusion | flops 2154299392 | bytes 7348224 | tf_op jit(solution)/shard_map/dot_general | solution.py:39
  215.1 23.0 %all-to-all-done.3 = bf16[32,64,1152]{2,1,0:T(8,128)(2,1)} async-done(((bf16[32,64,1152]{2,1,0:T(8,128)(2,1)}), bf16[32,64,1152]{2,1,0:T(8,128)(2,1)}, u32[]{:S(2)}, u32[]{:S(2)}) %all-to-all-start.3) | async-done | bytes 4718624 | tf_op jit(solution)/shard_map/all_to_all | solution.py:367
  239.1 5.2 %return.1 = (f32[192,1024]{1,0:T(8,128)S(1)}, bf16[192,1024]{1,0:T(8,128)(2,1)S(1)}, f32[1024,128]{1,0:T(8,128)S(1)}) custom-call(bf16[2048,1152]{1,0:T(8,128)(2,1)} %bitcast.58.back, bf16[192,2048]{1,0:T(8,128)(2,1)S(1)} %copy-done.6, f32[192,1024]{1,0:T(8,128)} %copy-done.7, bf16[192,1024]{1,0:T(8,128)(2,1)S(1)} %copy-done.24, ...), custom_call_target="tpu_custom_call" | custom-call | tf_op jit(solution)/shard_map/return/pallas_call | solution.py:54
  245.5 2.9 collective-permute-start.15
  248.5 5.5 %convolution_convert_fusion = bf16[1024,512]{1,0:T(8,128)(2,1)} fusion(bf16[2048,1024]{1,0:T(8,128)(2,1)} %bitcast.49.rows, bf16[2048,512]{1,0:T(8,128)(2,1)S(1)} %copy-done.45), kind=kOutput, calls=%fused_computation.22 | convolution fusion | flops 2148007936 | bytes 7340032 | tf_op jit(solution)/shard_map/dot_general | solution.py:39
  254.0 3.3 collective-permute-done.14
  257.3 8.2 %collective-permute-done.15 = bf16[192,1024]{1,0:T(8,128)(2,1)S(1)} collective-permute-done((bf16[192,1024]{1,0:T(8,128)(2,1)S(1)}, bf16[192,1024]{1,0:T(8,128)(2,1)S(1)}, u32[]{:S(2)}, u32[]{:S(2)}) %collective-permute-start.15) | collective-permute-done | bytes 393248 | tf_op jit(solution)/shard_map/ppermute | solution.py:341
  267.8 18.2 %attention_back.1 = (bf16[1024,896]{1,0:T(8,128)(2,1)}, bf16[768,1024]{1,0:T(8,128)(2,1)}) custom-call(s32[1]{0:T(128)} %copy.75.split, bf16[768,1024]{1,0:T(8,128)(2,1)} %copy-done.32, bf16[768,256]{1,0:T(8,128)(2,1)S(1)} %constant_dynamic-slice_fusion.gb_cols, bf16[256,1024]{1,0:T(8,128)(2,1)S(1)} %copy-done.10, ...), custom_call_target="tpu_custom_call" | custom-call | tf_op jit(solution)/shard_map/attention_back/pallas_call | solution.py:54
  286.0 2.9 copy.57
  288.9 9.9 %all-to-all-start.4 = ((bf16[128,8,896]{2,1,0:T(8,128)(2,1)}), bf16[128,8,896]{2,1,0:T(8,128)(2,1)}, u32[]{:S(2)}, u32[]{:S(2)}) async-start(bf16[128,8,896]{2,1,0:T(8,128)(2,1)} %bitcast.246), calls=%async_computation.4 | async-start | bytes 3670016 | tf_op jit(solution)/shard_map/all_to_all | solution.py:557
  302.3 3.2 collective-permute-start.24
  306.8 4.4 multiply_convert_fusion.1
  311.2 27.5 %collective-permute-done.23 = bf16[768,512]{1,0:T(8,128)(2,1)S(1)} collective-permute-done((bf16[768,512]{1,0:T(8,128)(2,1)S(1)}, bf16[768,512]{1,0:T(8,128)(2,1)S(1)}, u32[]{:S(2)}, u32[]{:S(2)}) %collective-permute-start.23) | collective-permute-done | bytes 786464 | tf_op jit(solution)/shard_map/ppermute | solution.py:341
  338.7 17.2 %collective-permute-done.24 = bf16[768,512]{1,0:T(8,128)(2,1)S(1)} collective-permute-done((bf16[768,512]{1,0:T(8,128)(2,1)S(1)}, bf16[768,512]{1,0:T(8,128)(2,1)S(1)}, u32[]{:S(2)}, u32[]{:S(2)}) %collective-permute-start.24) | collective-permute-done | bytes 786464 | tf_op jit(solution)/shard_map/ppermute | solution.py:341
  357.4 6.5 %all-to-all-start.2 = ((bf16[32,64,1024]{2,1,0:T(8,128)(2,1)}), bf16[32,64,1024]{2,1,0:T(8,128)(2,1)}, u32[]{:S(2)}, u32[]{:S(2)}) async-start(bf16[32,64,1024]{2,1,0:T(8,128)(2,1)} %bitcast.251), calls=%async_computation.2 | async-start | bytes 8388608 | tf_op jit(solution)/shard_map/all_to_all | solution.py:367
  365.0 1.8 convert_reduce_fusion
  367.0 49.7 %all-to-all-done.2 = bf16[32,64,1024]{2,1,0:T(8,128)(2,1)} async-done(((bf16[32,64,1024]{2,1,0:T(8,128)(2,1)}), bf16[32,64,1024]{2,1,0:T(8,128)(2,1)}, u32[]{:S(2)}, u32[]{:S(2)}) %all-to-all-start.2) | async-done | bytes 4194336 | tf_op jit(solution)/shard_map/all_to_all | solution.py:367
  418.1 6.6 %all-to-all-start.5 = ((bf16[32,8,3200]{2,1,0:T(8,128)(2,1)}), bf16[32,8,3200]{2,1,0:T(8,128)(2,1)}, u32[]{:S(2)}, u32[]{:S(2)}) async-start(bf16[32,8,3200]{2,1,0:T(8,128)(2,1)} %broadcast_in_dim.33), calls=%async_computation.5 | async-start | bytes 3276800 | tf_op jit(solution)/shard_map/all_to_all | solution.py:367
  425.5 2.3 slice_bitcast_fusion
  428.4 1.7 collective-permute-start.21
  430.1 2.0 collective-permute-start.22
  432.1 4.1 fusion.11
  436.3 12.6 %collective-permute-done.20 = bf16[192,1024]{1,0:T(8,128)(2,1)S(1)} collective-permute-done((bf16[192,1024]{1,0:T(8,128)(2,1)S(1)}, bf16[192,1024]{1,0:T(8,128)(2,1)S(1)}, u32[]{:S(2)}, u32[]{:S(2)}) %collective-permute-start.20) | collective-permute-done | bytes 393248 | tf_op jit(solution)/shard_map/ppermute | solution.py:341
  451.2 1.6 bitcast_convert_fusion
  (206 shorter events, 50.2 us)
Async XLA Ops:
  0.6 100.6 %copy-start = (bf16[1,512,1024]{2,1,0:T(8,128)(2,1)S(1)}, bf16[1,512,1024]{2,1,0:T(8,128)(2,1)}, u32[]{:S(2)}) copy-start(bf16[1,512,1024]{2,1,0:T(8,128)(2,1)} %param.24) | copy-start | bytes 3145732
  10.5 14.0 %copy-start.41 = (bf16[256]{0:T(256)(128)(2,1)S(1)}, bf16[256]{0:T(256)(128)(2,1)}, u32[]{:S(2)}) copy-start(bf16[256]{0:T(256)(128)(2,1)} %param.20) | copy-start | bytes 1540
  10.5 14.1 %copy-start.42 = (bf16[256]{0:T(256)(128)(2,1)S(1)}, bf16[256]{0:T(256)(128)(2,1)}, u32[]{:S(2)}) copy-start(bf16[256]{0:T(256)(128)(2,1)} %param.21) | copy-start | bytes 1540
  10.5 14.2 %copy-start.40 = (bf16[256,32]{0,1:T(8,128)(2,1)S(1)}, bf16[256,32]{0,1:T(8,128)(2,1)}, u32[]{:S(2)}) copy-start(bf16[256,32]{0,1:T(8,128)(2,1)} %param.19) | copy-start | bytes 49156
  10.5 14.4 %copy-start.38 = (bf16[256,512]{1,0:T(8,128)(2,1)S(1)}, bf16[256,512]{1,0:T(8,128)(2,1)}, u32[]{:S(2)}) copy-start(bf16[256,512]{1,0:T(8,128)(2,1)} %param.17) | copy-start | bytes 786436
  10.5 14.4 %copy-start.37 = (bf16[256,1024]{1,0:T(8,128)(2,1)S(1)}, bf16[256,1024]{1,0:T(8,128)(2,1)}, u32[]{:S(2)}) copy-start(bf16[256,1024]{1,0:T(8,128)(2,1)} %param.15) | copy-start | bytes 1572868
  10.5 14.5 %copy-start.39 = (bf16[256,512]{1,0:T(8,128)(2,1)S(1)}, bf16[256,512]{1,0:T(8,128)(2,1)}, u32[]{:S(2)}) copy-start(bf16[256,512]{1,0:T(8,128)(2,1)} %param.16) | copy-start | bytes 786436
  10.5 83.0 %all-to-all-start.1 = ((bf16[32,64,1152]{2,1,0:T(8,128)(2,1)}), bf16[32,64,1152]{2,1,0:T(8,128)(2,1)}, u32[]{:S(2)}, u32[]{:S(2)}) async-start(bf16[32,64,1152]{2,1,0:T(8,128)(2,1)} %bitcast.247), calls=%async_computation.1 | async-start | bytes 9437184 | tf_op jit(solution)/shard_map/all_to_all | solution.py:367
  18.9 26.6 %collective-permute-start.10 = (bf16[128,1024]{1,0:T(8,128)(2,1)}, bf16[128,1024]{1,0:T(8,128)(2,1)}, u32[]{:S(2)}, u32[]{:S(2)}) collective-permute-start(bf16[128,1024]{1,0:T(8,128)(2,1)} %constant_dynamic-slice_fusion.1), channel_id=1, source_target_pairs={{0,1},{1,2},{2,3},{3,0},{4,5},{5,6},{6,7},{7,4},{8,9},{9,10},{10,1... | collective-permute-start | bytes 786440 | tf_op jit(solution)/shard_map/ppermute | solution.py:341
  20.9 26.5 %collective-permute-start.11 = (bf16[128,1024]{1,0:T(8,128)(2,1)}, bf16[128,1024]{1,0:T(8,128)(2,1)}, u32[]{:S(2)}, u32[]{:S(2)}) collective-permute-start(bf16[128,1024]{1,0:T(8,128)(2,1)} %constant_dynamic-slice_fusion.1), channel_id=1, source_target_pairs={{0,2},{1,3},{2,0},{3,1},{4,6},{5,7},{6,4},{7,5},{8,10},{9,11},{10,... | collective-permute-start | bytes 786440 | tf_op jit(solution)/shard_map/ppermute | solution.py:341
  26.0 15.1 %copy-start.2 = (bf16[192,1024]{1,0:T(8,128)(2,1)S(1)}, bf16[192,1024]{1,0:T(8,128)(2,1)}, u32[]{:S(2)}) copy-start(bf16[192,1024]{1,0:T(8,128)(2,1)} %x_ref.1) | copy-start | bytes 1179652
  26.0 15.1 %collective-permute-start.4 = (bf16[128,640]{1,0:T(8,128)(2,1)}, bf16[128,640]{1,0:T(8,128)(2,1)}, u32[]{:S(2)}, u32[]{:S(2)}) collective-permute-start(bf16[128,640]{1,0:T(8,128)(2,1)} %get-tuple-element.174), channel_id=1, source_target_pairs={{0,2},{1,3},{2,0},{3,1},{4,6},{5,7},{6,4},{7,5},{8,10},{9,11},{10,... | collective-permute-start | bytes 491528 | tf_op jit(solution)/shard_map/ppermute | solution.py:341
  26.0 15.1 %collective-permute-start.5 = (bf16[128,640]{1,0:T(8,128)(2,1)}, bf16[128,640]{1,0:T(8,128)(2,1)}, u32[]{:S(2)}, u32[]{:S(2)}) collective-permute-start(bf16[128,640]{1,0:T(8,128)(2,1)} %get-tuple-element.175), channel_id=1, source_target_pairs={{0,3},{1,0},{2,1},{3,2},{4,7},{5,4},{6,5},{7,6},{8,11},{9,8},{10,9... | collective-permute-start | bytes 491528 | tf_op jit(solution)/shard_map/ppermute | solution.py:341
  28.1 15.6 %collective-permute-start.3 = (bf16[128,640]{1,0:T(8,128)(2,1)}, bf16[128,640]{1,0:T(8,128)(2,1)}, u32[]{:S(2)}, u32[]{:S(2)}) collective-permute-start(bf16[128,640]{1,0:T(8,128)(2,1)} %get-tuple-element.173), channel_id=1, source_target_pairs={{0,1},{1,2},{2,3},{3,0},{4,5},{5,6},{6,7},{7,4},{8,9},{9,10},{10,1... | collective-permute-start | bytes 491528 | tf_op jit(solution)/shard_map/ppermute | solution.py:341
  31.6 35.7 %copy-start.3 = (f32[768,128]{1,0:T(8,128)}, f32[768,128]{1,0:T(8,128)S(1)}, u32[]{:S(2)}) copy-start(f32[768,128]{1,0:T(8,128)S(1)} %get-tuple-element.181.sine) | copy-start | bytes 1179652
  31.6 18.9 %copy-start.36 = (bf16[1,128,1024]{2,1,0:T(8,128)(2,1)S(1)}, bf16[1,128,1024]{2,1,0:T(8,128)(2,1)}, u32[]{:S(2)}) copy-start(bf16[1,128,1024]{2,1,0:T(8,128)(2,1)} %fusion.44) | copy-start | bytes 786436
  41.0 9.5 %collective-permute-start.12 = (bf16[128,1024]{1,0:T(8,128)(2,1)}, bf16[128,1024]{1,0:T(8,128)(2,1)S(1)}, u32[]{:S(2)}, u32[]{:S(2)}) collective-permute-start(bf16[128,1024]{1,0:T(8,128)(2,1)} %constant_dynamic-slice_fusion.1), channel_id=1, source_target_pairs={{0,3},{1,0},{2,1},{3,2},{4,7},{5,4},{6,5},{7,6},{8,11},{9,8},{10,9... | collective-permute-start | bytes 786440 | tf_op jit(solution)/shard_map/ppermute | solution.py:341
  41.1 11.7 %collective-permute-start = (bf16[192,1024]{1,0:T(8,128)(2,1)S(1)}, bf16[192,1024]{1,0:T(8,128)(2,1)S(1)}, u32[]{:S(2)}, u32[]{:S(2)}) collective-permute-start(bf16[192,1024]{1,0:T(8,128)(2,1)S(1)} %copy-done.2), channel_id=1, source_target_pairs={{0,1},{1,2},{2,3},{3,0},{4,5},{5,6},{6,7},{7,4},{8,9},{9,10},{10,1... | collective-permute-start | bytes 1179656 | tf_op jit(solution)/shard_map/ppermute | solution.py:341
  43.6 17.0 %collective-permute-start.1 = (bf16[192,1024]{1,0:T(8,128)(2,1)S(1)}, bf16[192,1024]{1,0:T(8,128)(2,1)S(1)}, u32[]{:S(2)}, u32[]{:S(2)}) collective-permute-start(bf16[192,1024]{1,0:T(8,128)(2,1)S(1)} %copy-done.2), channel_id=1, source_target_pairs={{0,2},{1,3},{2,0},{3,1},{4,6},{5,7},{6,4},{7,5},{8,10},{9,11},{10,... | collective-permute-start | bytes 1179656 | tf_op jit(solution)/shard_map/ppermute | solution.py:341
  45.6 19.4 %collective-permute-start.2 = (bf16[192,1024]{1,0:T(8,128)(2,1)S(1)}, bf16[192,1024]{1,0:T(8,128)(2,1)S(1)}, u32[]{:S(2)}, u32[]{:S(2)}) collective-permute-start(bf16[192,1024]{1,0:T(8,128)(2,1)S(1)} %copy-done.2), channel_id=1, source_target_pairs={{0,3},{1,0},{2,1},{3,2},{4,7},{5,4},{6,5},{7,6},{8,11},{9,8},{10,9... | collective-permute-start | bytes 1179656 | tf_op jit(solution)/shard_map/ppermute | solution.py:341
  47.3 19.3 %collective-permute-start.6 = (bf16[4,128,640]{2,1,0:T(8,128)(2,1)S(1)}, bf16[4,128,640]{2,1,0:T(8,128)(2,1)S(1)}, u32[]{:S(2)}, u32[]{:S(2)}) collective-permute-start(bf16[4,128,640]{2,1,0:T(8,128)(2,1)S(1)} %bitcast.253), channel_id=1, source_target_pairs={{0,4},{4,0},{8,12},{12,8},{16,20},{20,16},{24,28},{28,24},{32,36},... | collective-permute-start | bytes 1966088 | tf_op jit(solution)/shard_map/ppermute | solution.py:360
  51.8 32.7 %collective-permute-start.13 = (bf16[4,128,1024]{2,1,0:T(8,128)(2,1)S(1)}, bf16[4,128,1024]{2,1,0:T(8,128)(2,1)S(1)}, u32[]{:S(2)}, u32[]{:S(2)}) collective-permute-start(bf16[4,128,1024]{2,1,0:T(8,128)(2,1)S(1)} %bitcast.249), channel_id=1, source_target_pairs={{0,4},{4,0},{8,12},{12,8},{16,20},{20,16},{24,28},{28,24},{32,36},... | collective-permute-start | bytes 3145736 | tf_op jit(solution)/shard_map/ppermute | solution.py:360
  66.9 12.9 %copy-start.1 = (bf16[4,2,128,640]{3,2,1,0:T(8,128)(2,1)}, bf16[4,2,128,640]{3,2,1,0:T(8,128)(2,1)S(1)}, u32[]{:S(2)}) copy-start(bf16[4,2,128,640]{3,2,1,0:T(8,128)(2,1)S(1)} %pad_maximum_fusion.8) | copy-start | bytes 3932164
  76.5 7.4 %collective-permute-start.7 = (bf16[192,256]{1,0:T(8,128)(2,1)S(1)}, bf16[192,256]{1,0:T(8,128)(2,1)S(1)}, u32[]{:S(2)}, u32[]{:S(2)}) collective-permute-start(bf16[192,256]{1,0:T(8,128)(2,1)S(1)} %get-tuple-element.163), channel_id=1, source_target_pairs={{0,1},{1,2},{2,3},{3,0},{4,5},{5,6},{6,7},{7,4},{8,9},{9,10},{10,1... | collective-permute-start | bytes 294920 | tf_op jit(solution)/shard_map/ppermute | solution.py:341
  76.6 7.4 %collective-permute-start.8 = (bf16[192,256]{1,0:T(8,128)(2,1)S(1)}, bf16[192,256]{1,0:T(8,128)(2,1)S(1)}, u32[]{:S(2)}, u32[]{:S(2)}) collective-permute-start(bf16[192,256]{1,0:T(8,128)(2,1)S(1)} %get-tuple-element.162), channel_id=1, source_target_pairs={{0,2},{1,3},{2,0},{3,1},{4,6},{5,7},{6,4},{7,5},{8,10},{9,11},{10,... | collective-permute-start | bytes 294920 | tf_op jit(solution)/shard_map/ppermute | solution.py:341
  79.5 4.9 %collective-permute-start.9 = (bf16[192,256]{1,0:T(8,128)(2,1)S(1)}, bf16[192,256]{1,0:T(8,128)(2,1)S(1)}, u32[]{:S(2)}, u32[]{:S(2)}) collective-permute-start(bf16[192,256]{1,0:T(8,128)(2,1)S(1)} %get-tuple-element.161), channel_id=1, source_target_pairs={{0,3},{1,0},{2,1},{3,2},{4,7},{5,4},{6,5},{7,6},{8,11},{9,8},{10,9... | collective-permute-start | bytes 294920 | tf_op jit(solution)/shard_map/ppermute | solution.py:341
  93.5 60.5 %all-to-all-start = ((bf16[32,64,1024]{2,1,0:T(8,128)(2,1)}), bf16[32,64,1024]{2,1,0:T(8,128)(2,1)}, u32[]{:S(2)}, u32[]{:S(2)}) async-start(bf16[32,64,1024]{2,1,0:T(8,128)(2,1)} %bitcast.252), calls=%async_computation | async-start | bytes 8388608 | tf_op jit(solution)/shard_map/all_to_all | solution.py:367
  172.4 65.7 %all-to-all-start.3 = ((bf16[32,64,1152]{2,1,0:T(8,128)(2,1)}), bf16[32,64,1152]{2,1,0:T(8,128)(2,1)}, u32[]{:S(2)}, u32[]{:S(2)}) async-start(bf16[32,64,1152]{2,1,0:T(8,128)(2,1)} %bitcast.248), calls=%async_computation.3 | async-start | bytes 9437184 | tf_op jit(solution)/shard_map/all_to_all | solution.py:367
  179.2 12.7 %collective-permute-start.17 = (bf16[768,256]{1,0:T(8,128)(2,1)S(1)}, bf16[768,256]{1,0:T(8,128)(2,1)S(1)}, u32[]{:S(2)}, u32[]{:S(2)}) collective-permute-start(bf16[768,256]{1,0:T(8,128)(2,1)S(1)} %copy-done.14), channel_id=1, source_target_pairs={{0,1},{1,2},{2,3},{3,0},{4,5},{5,6},{6,7},{7,4},{8,9},{9,10},{10,1... | collective-permute-start | bytes 1179656 | tf_op jit(solution)/shard_map/ppermute | solution.py:341
  180.2 20.5 %collective-permute-start.18 = (bf16[768,256]{1,0:T(8,128)(2,1)S(1)}, bf16[768,256]{1,0:T(8,128)(2,1)S(1)}, u32[]{:S(2)}, u32[]{:S(2)}) collective-permute-start(bf16[768,256]{1,0:T(8,128)(2,1)S(1)} %copy-done.14), channel_id=1, source_target_pairs={{0,2},{1,3},{2,0},{3,1},{4,6},{5,7},{6,4},{7,5},{8,10},{9,11},{10,... | collective-permute-start | bytes 1179656 | tf_op jit(solution)/shard_map/ppermute | solution.py:341
  183.1 17.7 %collective-permute-start.19 = (bf16[768,256]{1,0:T(8,128)(2,1)S(1)}, bf16[768,256]{1,0:T(8,128)(2,1)S(1)}, u32[]{:S(2)}, u32[]{:S(2)}) collective-permute-start(bf16[768,256]{1,0:T(8,128)(2,1)S(1)} %copy-done.14), channel_id=1, source_target_pairs={{0,3},{1,0},{2,1},{3,2},{4,7},{5,4},{6,5},{7,6},{8,11},{9,8},{10,9... | collective-permute-start | bytes 1179656 | tf_op jit(solution)/shard_map/ppermute | solution.py:341
  209.3 28.8 %copy-start.6 = (bf16[192,2048]{1,0:T(8,128)(2,1)S(1)}, bf16[192,2048]{1,0:T(8,128)(2,1)}, u32[]{:S(2)}) copy-start(bf16[192,2048]{1,0:T(8,128)(2,1)} %copy-done.5) | copy-start | bytes 2359300
  209.3 28.8 %copy-start.12 = (bf16[192,1024]{1,0:T(8,128)(2,1)S(1)}, bf16[192,1024]{1,0:T(8,128)(2,1)}, u32[]{:S(2)}) copy-start(bf16[192,1024]{1,0:T(8,128)(2,1)} %cot.3) | copy-start | bytes 1179652
  239.1 9.3 %copy-start.45 = (bf16[2048,512]{1,0:T(8,128)(2,1)S(1)}, bf16[2048,512]{1,0:T(8,128)(2,1)}, u32[]{:S(2)}) copy-start(bf16[2048,512]{1,0:T(8,128)(2,1)} %get-tuple-element.57) | copy-start | bytes 6291460
  244.4 9.7 %copy-start.21 = (f32[192,1024]{1,0:T(8,128)}, f32[192,1024]{1,0:T(8,128)S(1)}, u32[]{:S(2)}) copy-start(f32[192,1024]{1,0:T(8,128)S(1)} %get-tuple-element.47) | copy-start | bytes 2359300
  244.4 12.9 %collective-permute-start.14 = (bf16[192,1024]{1,0:T(8,128)(2,1)S(1)}, bf16[192,1024]{1,0:T(8,128)(2,1)S(1)}, u32[]{:S(2)}, u32[]{:S(2)}) collective-permute-start(bf16[192,1024]{1,0:T(8,128)(2,1)S(1)} %get-tuple-element.48), channel_id=1, source_target_pairs={{0,1},{1,2},{2,3},{3,0},{4,5},{5,6},{6,7},{7,4},{8,9},{9,10},{10,1... | collective-permute-start | bytes 1179656 | tf_op jit(solution)/shard_map/ppermute | solution.py:341
  245.5 20.0 %collective-permute-start.15 = (bf16[192,1024]{1,0:T(8,128)(2,1)S(1)}, bf16[192,1024]{1,0:T(8,128)(2,1)S(1)}, u32[]{:S(2)}, u32[]{:S(2)}) collective-permute-start(bf16[192,1024]{1,0:T(8,128)(2,1)S(1)} %get-tuple-element.48), channel_id=1, source_target_pairs={{0,2},{1,3},{2,0},{3,1},{4,6},{5,7},{6,4},{7,5},{8,10},{9,11},{10,... | collective-permute-start | bytes 1179656 | tf_op jit(solution)/shard_map/ppermute | solution.py:341
  248.4 17.1 %collective-permute-start.16 = (bf16[192,1024]{1,0:T(8,128)(2,1)S(1)}, bf16[192,1024]{1,0:T(8,128)(2,1)S(1)}, u32[]{:S(2)}, u32[]{:S(2)}) collective-permute-start(bf16[192,1024]{1,0:T(8,128)(2,1)S(1)} %get-tuple-element.48), channel_id=1, source_target_pairs={{0,3},{1,0},{2,1},{3,2},{4,7},{5,4},{6,5},{7,6},{8,11},{9,8},{10,9... | collective-permute-start | bytes 1179656 | tf_op jit(solution)/shard_map/ppermute | solution.py:341
  288.9 68.5 %all-to-all-start.4 = ((bf16[128,8,896]{2,1,0:T(8,128)(2,1)}), bf16[128,8,896]{2,1,0:T(8,128)(2,1)}, u32[]{:S(2)}, u32[]{:S(2)}) async-start(bf16[128,8,896]{2,1,0:T(8,128)(2,1)} %bitcast.246), calls=%async_computation.4 | async-start | bytes 3670016 | tf_op jit(solution)/shard_map/all_to_all | solution.py:557
  301.2 37.5 %collective-permute-start.23 = (bf16[768,512]{1,0:T(8,128)(2,1)S(1)}, bf16[768,512]{1,0:T(8,128)(2,1)S(1)}, u32[]{:S(2)}, u32[]{:S(2)}) collective-permute-start(bf16[768,512]{1,0:T(8,128)(2,1)S(1)} %get-tuple-element.116), channel_id=1, source_target_pairs={{0,1},{1,2},{2,3},{3,0},{4,5},{5,6},{6,7},{7,4},{8,9},{9,10},{10,1... | collective-permute-start | bytes 2359304 | tf_op jit(solution)/shard_map/ppermute | solution.py:341
  302.3 53.6 %collective-permute-start.24 = (bf16[768,512]{1,0:T(8,128)(2,1)S(1)}, bf16[768,512]{1,0:T(8,128)(2,1)S(1)}, u32[]{:S(2)}, u32[]{:S(2)}) collective-permute-start(bf16[768,512]{1,0:T(8,128)(2,1)S(1)} %get-tuple-element.118), channel_id=1, source_target_pairs={{0,2},{1,3},{2,0},{3,1},{4,6},{5,7},{6,4},{7,5},{8,10},{9,11},{10,... | collective-permute-start | bytes 2359304 | tf_op jit(solution)/shard_map/ppermute | solution.py:341
  305.5 50.4 %collective-permute-start.25 = (bf16[768,512]{1,0:T(8,128)(2,1)S(1)}, bf16[768,512]{1,0:T(8,128)(2,1)S(1)}, u32[]{:S(2)}, u32[]{:S(2)}) collective-permute-start(bf16[768,512]{1,0:T(8,128)(2,1)S(1)} %get-tuple-element.117), channel_id=1, source_target_pairs={{0,3},{1,0},{2,1},{3,2},{4,7},{5,4},{6,5},{7,6},{8,11},{9,8},{10,9... | collective-permute-start | bytes 2359304 | tf_op jit(solution)/shard_map/ppermute | solution.py:341
  357.4 59.3 %all-to-all-start.2 = ((bf16[32,64,1024]{2,1,0:T(8,128)(2,1)}), bf16[32,64,1024]{2,1,0:T(8,128)(2,1)}, u32[]{:S(2)}, u32[]{:S(2)}) async-start(bf16[32,64,1024]{2,1,0:T(8,128)(2,1)} %bitcast.251), calls=%async_computation.2 | async-start | bytes 8388608 | tf_op jit(solution)/shard_map/all_to_all | solution.py:367
  418.1 33.1 %all-to-all-start.5 = ((bf16[32,8,3200]{2,1,0:T(8,128)(2,1)}), bf16[32,8,3200]{2,1,0:T(8,128)(2,1)}, u32[]{:S(2)}, u32[]{:S(2)}) async-start(bf16[32,8,3200]{2,1,0:T(8,128)(2,1)} %broadcast_in_dim.33), calls=%async_computation.5 | async-start | bytes 3276800 | tf_op jit(solution)/shard_map/all_to_all | solution.py:367
  427.9 20.9 %collective-permute-start.20 = (bf16[192,1024]{1,0:T(8,128)(2,1)S(1)}, bf16[192,1024]{1,0:T(8,128)(2,1)S(1)}, u32[]{:S(2)}, u32[]{:S(2)}) collective-permute-start(bf16[192,1024]{1,0:T(8,128)(2,1)S(1)} %get-tuple-element.125), channel_id=1, source_target_pairs={{0,1},{1,2},{2,3},{3,0},{4,5},{5,6},{6,7},{7,4},{8,9},{9,10},{10,1... | collective-permute-start | bytes 1179656 | tf_op jit(solution)/shard_map/ppermute | solution.py:341
  428.4 20.5 %collective-permute-start.21 = (bf16[192,1024]{1,0:T(8,128)(2,1)S(1)}, bf16[192,1024]{1,0:T(8,128)(2,1)S(1)}, u32[]{:S(2)}, u32[]{:S(2)}) collective-permute-start(bf16[192,1024]{1,0:T(8,128)(2,1)S(1)} %get-tuple-element.127), channel_id=1, source_target_pairs={{0,2},{1,3},{2,0},{3,1},{4,6},{5,7},{6,4},{7,5},{8,10},{9,11},{10,... | collective-permute-start | bytes 1179656 | tf_op jit(solution)/shard_map/ppermute | solution.py:341
  430.1 19.4 %collective-permute-start.22 = (bf16[192,1024]{1,0:T(8,128)(2,1)S(1)}, bf16[192,1024]{1,0:T(8,128)(2,1)S(1)}, u32[]{:S(2)}, u32[]{:S(2)}) collective-permute-start(bf16[192,1024]{1,0:T(8,128)(2,1)S(1)} %get-tuple-element.126), channel_id=1, source_target_pairs={{0,3},{1,0},{2,1},{3,2},{4,7},{5,4},{6,5},{7,6},{8,11},{9,8},{10,9... | collective-permute-start | bytes 1179656 | tf_op jit(solution)/shard_map/ppermute | solution.py:341
  436.3 13.6 %copy-start.22 = (f32[192,1024]{1,0:T(8,128)S(1)}, f32[192,1024]{1,0:T(8,128)}, u32[]{:S(2)}) copy-start(f32[192,1024]{1,0:T(8,128)} %copy-done.21) | copy-start | bytes 2359300
  (31 other events, 89.0 us)
